TPU v7x, 32 devices: a whole 2x2x4 slice. The times are simulated.
32 devices in a mesh: tau: 2 (over x), blk: 16 (over z, y, core).
Axes of the slice: x: 2, y: 2, z: 4, core: 2. Of those that a mesh axis runs over, the one named last changes fastest.
Arguments:
- three_center: bfloat16 [16, 128, 128, 128], P('blk'), may hold values from -0.59765625 to 0.59765625
- green_blocks: bfloat16 [2, 128, 2048], P('tau', 'blk'), may hold values from -0.5 to 0.5
- block_owner: int32 [768], P('blk'), may hold values from 0 to 15, as said below
- block_slot: int32 [768], P('blk'), may hold values from 0 to 7
- fold_weights: float32 [2, 2], P(None, 'tau'), may hold values from -1 to 1
Outputs:
- chi_freq: float32 [2, 2048, 384], P('tau', 'blk')
Inputs may be any that keep to these rules, and one draw needn't show every extreme that they name: `block_owner`: among the 48 entries of each auxiliary block, no owner appears more than 6 times, and one owner appears exactly 6 times in the entries of every auxiliary block.
All inputs are finite; a program needn't handle non-finite values.
Results may differ from a plain program's by a relative error of at most 0.0041.
Values may be sent and summed in bfloat16 or wider, within the bound.
A program may use at most 128 MiB of HBM per device.

v0:
```python
import jax
import jax.numpy as jnp
from jax import lax
from jax.sharding import PartitionSpec as P

AB = 32
NS = 4
HALF = 1


def from_behind(value, axis, by):
    size = lax.axis_size(axis)
    return lax.ppermute(value, axis, [(i, (i + by) % size) for i in range(size)])


def green_pair(blocks):
    blocks = blocks.reshape(NS, NS, 2, AB, AB)
    occupied = blocks[:, :, 0].transpose(0, 2, 1, 3).reshape(NS * AB, NS * AB)
    virtual = blocks[:, :, 1].transpose(0, 2, 1, 3).reshape(NS * AB, NS * AB)
    return (occupied, virtual)


def transform(occupied, virtual, source):
    region = source.shape[0]
    aux_width = source.shape[2]
    halfway = jnp.einsum("sn,mnb->msb", virtual, source, preferred_element_type=jnp.float32).astype(
        jnp.bfloat16
    )
    image_block = jnp.dot(
        occupied, halfway.reshape(region, region * aux_width), preferred_element_type=jnp.float32
    )
    return image_block.astype(jnp.bfloat16).reshape(region, region, aux_width)


def pair_block(partner, image_block):
    region = partner.shape[0]
    aux_width = partner.shape[2]
    flat_image = image_block.reshape(region * region, aux_width)
    flat_partner = partner.reshape(region * region, aux_width)
    product = lax.dot_general(
        flat_image, flat_partner, (((0,), (0,)), ((), ())), preferred_element_type=jnp.float32
    )
    return -2.0 * product


def local(three_center, green_blocks, block_owner, block_slot, fold_weights):
    source = three_center[0]
    local_table = green_blocks[0]
    devices = lax.axis_size("blk")
    requests = block_owner.shape[0]
    per_slot = NS * NS
    capacity = 2 * ((requests + devices - 1) // devices)
    owner_match = (block_owner[:, None] == jnp.arange(devices, dtype=jnp.int32)[None, :]).astype(
        jnp.int32
    )
    position = jnp.sum(jnp.cumsum(owner_match, axis=0) * owner_match, axis=1) - 1
    outgoing = jnp.zeros((devices, capacity), jnp.int32).at[block_owner, position].set(block_slot)
    found_blocks = jnp.take(
        local_table,
        lax.all_to_all(outgoing, "blk", split_axis=0, concat_axis=0, tiled=True),
        axis=0,
    )
    replies = lax.all_to_all(found_blocks, "blk", split_axis=0, concat_axis=0, tiled=True)
    fetched = replies[block_owner, position]
    partners_total = 2 * HALF + 1
    pieces = []
    for slot_index in range(partners_total):
        occupied, virtual = green_pair(fetched[slot_index * per_slot : (slot_index + 1) * per_slot])
        image_block = transform(occupied, virtual, source)
        if slot_index == HALF:
            partner = source
        else:
            partner = from_behind(source, "blk", HALF - slot_index)
        pieces.append(pair_block(partner, image_block))
    chi_time = jnp.concatenate(pieces, axis=1)
    column_weights = fold_weights[:, 0]
    return lax.psum_scatter(
        column_weights[:, None, None] * chi_time[None], "tau", scatter_dimension=0, tiled=True
    )


def solution(mesh):
    return jax.shard_map(
        local,
        mesh=mesh,
        in_specs=(
            P("blk", None, None, None),
            P("tau", "blk", None),
            P("blk"),
            P("blk"),
            P(None, "tau"),
        ),
        out_specs=P("tau", "blk", None),
        check_vma=False,
    )
```

profile of v0, /device:TPU:0, one launch (start us, length us, event | category | flops | bytes accessed | tf_op | source)
XLA Modules:
  0.0 180.9 jit_solution(14234872959371672290)
XLA Ops:
  6.5 0.7 fusion.6
  7.3 0.8 select_reduce_fusion
  8.2 0.7 fusion.10
  8.9 4.4 %scatter_fusion = s32[16,6]{0,1:T(8,128)S(1)} fusion(s32[16,6]{0,1:T(8,128)S(1)} %broadcast_in_dim.24, s32[48]{0:T(128)S(1)} %get-tuple-element.15, s32[48]{0:T(128)} %param.8), kind=kCustom, calls=%fused_computation.2 | custom fusion | bytes 960 | tf_op jit(solution)/shard_map/scatter | solution.py:57
  13.4 13.6 %all_to_all.20 = s32[16,1,6]{2,1,0:T(1,128)S(1)} all-to-all(s32[16,1,6]{2,1,0:T(1,128)S(1)} %copy.21), channel_id=1, replica_groups=mesh['tau'=2,'blk'=16] {'blk'}, dimensions={0} | all-to-all | bytes 768 | tf_op jit(solution)/shard_map/all_to_all | solution.py:60
  27.3 0.8 gather_fusion
  28.4 1.0 broadcast_select_fusion
  29.4 3.6 %all-to-all-start.1 = ((bf16[16,6,2048]{2,1,0:T(8,128)(2,1)}), bf16[16,6,2048]{2,1,0:T(8,128)(2,1)S(1)}, u32[]{:S(2)}, u32[]{:S(2)}) async-start(bf16[16,6,2048]{2,1,0:T(8,128)(2,1)} %broadcast_select_fusion), calls=%async_computation.1 | async-start | bytes 1048576 | tf_op jit(solution)/shard_map/all_to_all | solution.py:63
  33.0 0.3 collective-permute-start
  33.4 4.2 %collective-permute-start.1 = (bf16[128,128,128]{2,1,0:T(8,128)(2,1)}, bf16[128,128,128]{2,1,0:T(8,128)(2,1)}, u32[]{:S(2)}, u32[]{:S(2)}) collective-permute-start(bf16[128,128,128]{2,1,0:T(8,128)(2,1)} %bitcast.109), channel_id=1, source_target_pairs={{0,15},{1,0},{2,1},{3,2},{4,3},{5,4},{6,5},{7,6},{8,7},{9,8},{10,9... | collective-permute-start | bytes 12582920 | tf_op jit(solution)/shard_map/ppermute | solution.py:13
  37.5 10.4 %all-to-all-done.1 = bf16[16,6,2048]{2,1,0:T(8,128)(2,1)S(1)} async-done(((bf16[16,6,2048]{2,1,0:T(8,128)(2,1)}), bf16[16,6,2048]{2,1,0:T(8,128)(2,1)S(1)}, u32[]{:S(2)}, u32[]{:S(2)}) %all-to-all-start.1) | async-done | bytes 393248 | tf_op jit(solution)/shard_map/all_to_all | solution.py:63
  47.9 0.2 copy.26
  48.1 1.5 gather_fusion.1
  49.7 0.2 reshape.101
  49.9 0.1 copy_bitcast_fusion.4
  50.2 5.4 %convolution_convert_fusion.5 = bf16[128,128,128]{2,0,1:T(8,128)(2,1)} fusion(bf16[128,128,1]{1,0,2:T(8,128)(2,1)S(1)} %reshape.136, bf16[1,128,128,128]{3,2,1,0:T(8,128)(2,1)} %param.5), kind=kOutput, calls=%fused_computation.14 | convolution fusion | flops 538968064 | bytes 8421376 | tf_op jit(solution)/shard_map/sn,mnb->msb/dot_general | solution.py:26
  55.7 7.3 %convolution_convert_fusion.2 = bf16[128,16384]{1,0:T(8,128)(2,1)} fusion(bf16[128,128]{1,0:T(8,128)(2,1)S(1)} %reshape.102, bf16[16,8,128,128]{3,2,1,0:T(8,128)(2,1)} %bitcast.111), kind=kOutput, calls=%fused_computation.5 | convolution fusion | flops 538968064 | bytes 8421376 | tf_op jit(solution)/shard_map/dot_general | solution.py:29
  63.0 7.4 %reshape_reshape.9 = bf16[16384,128]{1,0:T(8,128)(2,1)} reshape(bf16[128,16384]{1,0:T(8,128)(2,1)} %convolution_convert_fusion.2) | data formatting | bytes 8388608 | tf_op jit(solution)/shard_map/reshape;reshape | solution.py:38
  70.5 0.2 reshape.110
  70.7 0.1 copy_bitcast_fusion
  71.1 3.4 %convolution_convert_fusion.3 = bf16[128,128,128]{2,0,1:T(8,128)(2,1)S(1)} fusion(bf16[128,128,1]{1,0,2:T(8,128)(2,1)S(1)} %reshape.138, bf16[1,128,128,128]{3,2,1,0:T(8,128)(2,1)} %param.5), kind=kOutput, calls=%fused_computation.12 | convolution fusion | flops 538968064 | bytes 8421376 | tf_op jit(solution)/shard_map/sn,mnb->msb/dot_general | solution.py:26
  74.5 5.2 %convolution_convert_fusion = bf16[128,16384]{1,0:T(8,128)(2,1)} fusion(bf16[128,128]{1,0:T(8,128)(2,1)S(1)} %reshape.111, bf16[16,8,128,128]{3,2,1,0:T(8,128)(2,1)S(1)} %bitcast.112), kind=kOutput, calls=%fused_computation.3 | convolution fusion | flops 538968064 | bytes 8421376 | tf_op jit(solution)/shard_map/dot_general | solution.py:29
  79.7 7.4 %reshape_reshape.11 = bf16[16384,128]{1,0:T(8,128)(2,1)} reshape(bf16[128,16384]{1,0:T(8,128)(2,1)} %convolution_convert_fusion) | data formatting | bytes 8388608 | tf_op jit(solution)/shard_map/reshape;reshape | solution.py:38
  87.1 0.2 reshape.106
  87.7 3.4 %convolution_convert_fusion.4 = bf16[128,128,128]{2,0,1:T(8,128)(2,1)S(1)} fusion(bf16[128,128,1]{1,0,2:T(8,128)(2,1)S(1)} %reshape.137, bf16[1,128,128,128]{3,2,1,0:T(8,128)(2,1)} %param.5), kind=kOutput, calls=%fused_computation.13 | convolution fusion | flops 538968064 | bytes 8421376 | tf_op jit(solution)/shard_map/sn,mnb->msb/dot_general | solution.py:26
  91.1 5.2 %convolution_convert_fusion.1 = bf16[128,16384]{1,0:T(8,128)(2,1)} fusion(bf16[128,128]{1,0:T(8,128)(2,1)S(1)} %reshape.107, bf16[16,8,128,128]{3,2,1,0:T(8,128)(2,1)S(1)} %bitcast.113), kind=kOutput, calls=%fused_computation.4 | convolution fusion | flops 538968064 | bytes 8421376 | tf_op jit(solution)/shard_map/dot_general | solution.py:29
  96.3 7.5 %reshape_reshape.10 = bf16[16384,128]{1,0:T(8,128)(2,1)} reshape(bf16[128,16384]{1,0:T(8,128)(2,1)} %convolution_convert_fusion.1) | data formatting | bytes 8388608 | tf_op jit(solution)/shard_map/reshape;reshape | solution.py:38
  103.7 4.9 %convolution_multiply_fusion.1 = f32[128,128]{0,1:T(8,128)S(1)} fusion(bf16[16384,128]{1,0:T(8,128)(2,1)} %reshape_reshape.10, bf16[16384,128]{1,0:T(8,128)(2,1)} %bitcast.110), kind=kOutput, calls=%fused_computation.16 | convolution fusion | flops 536887296 | bytes 8454144 | tf_op jit(solution)/shard_map/dot_general | solution.py:40
  108.7 3.7 %convolution_multiply_fusion.2 = f32[128,128]{0,1:T(8,128)S(1)} fusion(bf16[16384,128]{1,0:T(8,128)(2,1)S(1)} %copy-done.1, bf16[16384,128]{1,0:T(8,128)(2,1)} %bitcast.16), kind=kOutput, calls=%fused_computation.17 | convolution fusion | flops 536887296 | bytes 8454144 | tf_op jit(solution)/shard_map/dot_general | solution.py:40
  112.4 3.5 %convolution_multiply_fusion = f32[128,128]{0,1:T(8,128)S(1)} fusion(bf16[16384,128]{1,0:T(8,128)(2,1)S(1)} %copy-done.2, bf16[16384,128]{1,0:T(8,128)(2,1)} %bitcast.28), kind=kOutput, calls=%fused_computation.15 | convolution fusion | flops 536887296 | bytes 8454144 | tf_op jit(solution)/shard_map/dot_general | solution.py:40
  116.1 0.8 broadcast_multiply_fusion
  117.0 57.1 %reduce-scatter.2.cloned.1.call-done = f32[1,128,384]{2,1,0:T(8,128)} async-done(((f32[2,128,384]{2,1,0:T(8,128)}), f32[1,128,384]{2,1,0:T(8,128)}) %reduce-scatter.2.cloned.1.call-update) | async-done | bytes 196624 | tf_op jit(solution)/shard_map/reduce_scatter | solution.py:77
  (37 shorter events, 1.9 us)
Async XLA Ops:
  6.5 20.7 %copy-start = (bf16[1,8,2048]{2,1,0:T(8,128)(2,1)S(1)}, bf16[1,8,2048]{2,1,0:T(8,128)(2,1)}, u32[]{:S(2)}) copy-start(bf16[1,8,2048]{2,1,0:T(8,128)(2,1)} %param.6) | copy-start | bytes 98308
  29.4 18.5 %all-to-all-start.1 = ((bf16[16,6,2048]{2,1,0:T(8,128)(2,1)}), bf16[16,6,2048]{2,1,0:T(8,128)(2,1)S(1)}, u32[]{:S(2)}, u32[]{:S(2)}) async-start(bf16[16,6,2048]{2,1,0:T(8,128)(2,1)} %broadcast_select_fusion), calls=%async_computation.1 | async-start | bytes 1048576 | tf_op jit(solution)/shard_map/all_to_all | solution.py:63
  33.0 141.1 %reduce-scatter.2.cloned.1.call-start = ((), (), s32[]{:S(2)}) async-start(), calls=%async_computation.3 | async-start | bytes 589824 | tf_op jit(solution)/shard_map/reduce_scatter | solution.py:77
  33.0 75.7 %collective-permute-start = (bf16[128,128,128]{2,1,0:T(8,128)(2,1)}, bf16[128,128,128]{2,1,0:T(8,128)(2,1)}, u32[]{:S(2)}, u32[]{:S(2)}) collective-permute-start(bf16[128,128,128]{2,1,0:T(8,128)(2,1)} %bitcast.108), channel_id=1, source_target_pairs={{0,1},{1,2},{2,3},{3,4},{4,5},{5,6},{6,7},{7,8},{8,9},{9,10},{10,1... | collective-permute-start | bytes 12582920 | tf_op jit(solution)/shard_map/ppermute | solution.py:13
  33.4 79.0 %collective-permute-start.1 = (bf16[128,128,128]{2,1,0:T(8,128)(2,1)}, bf16[128,128,128]{2,1,0:T(8,128)(2,1)}, u32[]{:S(2)}, u32[]{:S(2)}) collective-permute-start(bf16[128,128,128]{2,1,0:T(8,128)(2,1)} %bitcast.109), channel_id=1, source_target_pairs={{0,15},{1,0},{2,1},{3,2},{4,3},{5,4},{6,5},{7,6},{8,7},{9,8},{10,9... | collective-permute-start | bytes 12582920 | tf_op jit(solution)/shard_map/ppermute | solution.py:13
  103.7 5.0 %copy-start.1 = (bf16[16384,128]{1,0:T(8,128)(2,1)S(1)}, bf16[16384,128]{1,0:T(8,128)(2,1)}, u32[]{:S(2)}) copy-start(bf16[16384,128]{1,0:T(8,128)(2,1)} %reshape_reshape.9) | copy-start | bytes 12582916
  108.7 3.7 %copy-start.2 = (bf16[16384,128]{1,0:T(8,128)(2,1)S(1)}, bf16[16384,128]{1,0:T(8,128)(2,1)}, u32[]{:S(2)}) copy-start(bf16[16384,128]{1,0:T(8,128)(2,1)} %reshape_reshape.11) | copy-start | bytes 12582916
  112.4 3.7 %copy-start.3 = (f32[2,1]{0,1:T(1,128)S(1)}, f32[2,1]{0,1:T(1,128)}, u32[]{:S(2)}) copy-start(f32[2,1]{0,1:T(1,128)} %param.9) | copy-start | bytes 28
Sparse Core Ops, SparseCore 0:
  117.1 56.9 reduce-scatter.1
where the time goes:
time: 182 us; the launch traced here: 181 us
  waiting for transfers between devices  67.5 us (37%)
  matrix products  42 us (23%)
  local copies, waits for them, and re-layouts  31.9 us (18%)
  between operations  13.7 us (8%)
  blocking collectives  13.6 us (7%)
  starting transfers between devices  8.11 us (4%)
  other arithmetic  4.15 us (2%)
    reduce_scatter x1, waiting for transfers between devices, local(): lax.psum_scatter(column_weights[:, None, None] * chi_time[None], 'tau', s...  57.1 us
    another operation x3, local copies, waits for them, and re-layouts, pair_block(): flat_image = image_block.reshape(region * region, aux_width)  22.2 us
    dot_general x3, matrix products, transform(): jnp.dot(occupied, halfway.reshape(region, region * aux_width), preferred_...  17.6 us
    all_to_all x1, blocking collectives, local(): lax.all_to_all(outgoing, 'blk', split_axis=0, concat_axis=0, tiled=True)  13.6 us
    dot_general x3, matrix products, transform(): jnp.einsum('sn,mnb->msb', virtual, source, preferred_element_type=jnp.flo...  12.2 us
    dot_general x3, matrix products, pair_block(): lax.dot_general(flat_image, flat_partner, (((0,), (0,)), ((), ())), prefe...  12.1 us
    all_to_all x1, waiting for transfers between devices, local(): lax.all_to_all(found_blocks, 'blk', split_axis=0, concat_axis=0, tiled=True)  10.4 us
    ppermute x2, starting transfers between devices, from_behind(): lax.ppermute(value, axis, [(i, (i + by) % size) for i in range(size)])  4.49 us
  transfers between devices with their start and end apart: 4, of which 2 were waited for; matrix products, arithmetic and copies ran while one was open for 36% of the time, Pallas kernels for 0%

commit v1 on v0

v1 whole, which is shorter than its diff:
```python
import jax
import jax.numpy as jnp
from jax import lax
from jax.sharding import PartitionSpec as P

AB = 32
NS = 4
HALF = 1


def green_pairs(blocks):
    count = blocks.shape[0] // (NS * NS)
    blocks = blocks.reshape(count, NS, NS, 2, AB, AB).transpose(3, 0, 1, 4, 2, 5)
    return blocks.reshape(2, count, NS * AB, NS * AB)


def transform(left, right, source):
    halfway = jnp.einsum("sn,mnb->smb", right, source, preferred_element_type=jnp.float32).astype(
        jnp.bfloat16
    )
    return jnp.einsum("lm,smb->slb", left, halfway, preferred_element_type=jnp.float32).astype(
        jnp.bfloat16
    )


def contract(first, second):
    width = first.shape[2]
    return lax.dot_general(
        first.reshape(-1, width),
        second.reshape(-1, width),
        (((0,), (0,)), ((), ())),
        preferred_element_type=jnp.float32,
    )


def exchange(chi, weights, step):
    taus = lax.axis_size("tau")
    blks = lax.axis_size("blk")
    t = lax.axis_index("tau")
    total = None
    for shift in range(taus):
        target = lax.rem(t + shift, taus)
        piece = lax.dynamic_index_in_dim(weights, target, 0, keepdims=False) * chi
        if shift or step:
            perm = [
                (i * blks + j, ((i + shift) % taus) * blks + (j + step) % blks)
                for i in range(taus)
                for j in range(blks)
            ]
            piece = lax.ppermute(piece, ("tau", "blk"), perm)
        total = piece if total is None else total + piece
    return total


def local(three_center, green_blocks, block_owner, block_slot, fold_weights):
    source = three_center[0]
    devices = lax.axis_size("blk")
    per_slot = NS * NS
    ahead = [(i, (i - 1) % devices) for i in range(devices)]
    ids = block_owner * green_blocks.shape[1] + block_slot
    table = lax.all_gather(green_blocks[0], "blk", axis=0, tiled=True)
    next_ids = lax.ppermute(ids[:per_slot], "blk", ahead)
    used = jnp.concatenate([next_ids, ids[per_slot:]])
    fetched = table.at[used].get(mode="promise_in_bounds")
    flipped = source.transpose(1, 0, 2)
    partner = lax.ppermute(flipped, "blk", ahead)
    occupied, virtual = green_pairs(fetched)
    weights = fold_weights[:, 0] * -2.0
    own = transform(occupied[1], virtual[1], source)
    down = transform(occupied[0].T, virtual[0].T, source)
    up = transform(occupied[2], virtual[2], source)
    out_own = exchange(contract(own, flipped), weights, 0)
    out_down = exchange(contract(partner, down), weights, 1)
    out_up = exchange(contract(up, partner), weights, 0)
    return jnp.concatenate([out_down, out_own, out_up], axis=1)[None]


def solution(mesh):
    return jax.shard_map(
        local,
        mesh=mesh,
        in_specs=(
            P("blk", None, None, None),
            P("tau", "blk", None),
            P("blk"),
            P("blk"),
            P(None, "tau"),
        ),
        out_specs=P("tau", "blk", None),
        check_vma=False,
    )
```

time: 182 us -> 135 us (0.74)
  waiting for transfers between devices: 67.5 us -> 6.32 us
  blocking collectives: 13.6 us -> 63 us
  local copies, waits for them, and re-layouts: 31.9 us -> 11.6 us
  between operations: 13.7 us -> 0.2 us
    all_gather x0 -> x1, blocking collectives: none -> 63 us  [local(): table = lax.all_gather(green_blocks[0], 'blk', axis=0, tiled=True)]
    reduce_scatter x1 -> x0, waiting for transfers between devices: 57.1 us -> none  [local(): lax.psum_scatter(column_weights[:, None, None] * chi_time[None], 'tau', s...]
    another operation x3 -> x0, local copies, waits for them, and re-layouts: 22.2 us -> none  [pair_block(): flat_image = image_block.reshape(region * region, aux_width)]
    all_to_all x1 -> x0, blocking collectives: 13.6 us -> none  [local(): lax.all_to_all(outgoing, 'blk', split_axis=0, concat_axis=0, tiled=True)]
    all_to_all x1 -> x0, waiting for transfers between devices: 10.4 us -> none  [local(): lax.all_to_all(found_blocks, 'blk', split_axis=0, concat_axis=0, tiled=True)]
    unnamed x8 -> x11, local copies, waits for them, and re-layouts: 0.02 us -> 6.92 us
    ppermute x2 -> x6, waiting for transfers between devices: 0.01 us -> 6.32 us  [the longest x4 6.32 us: exchange(): piece = lax.ppermute(piece, ('tau', 'blk'), perm)]
    ppermute x2 -> x6, starting transfers between devices: 4.49 us -> 9.33 us  [the longest x1 5.45 us: local(): partner = lax.ppermute(flipped, 'blk', ahead)]
  transfers between devices with their start and end apart: 4 -> 6, of which waited for: 2 -> 3; matrix products, arithmetic and copies ran while one was open for 36% -> 22% of each run, Pallas kernels for 0% -> 0%
where the time goes in v1:
time: 135 us
  blocking collectives  63 us (47%)
  matrix products  41.9 us (31%)
  local copies, waits for them, and re-layouts  11.6 us (9%)
  starting transfers between devices  9.33 us (7%)
  waiting for transfers between devices  6.32 us (5%)
  other arithmetic  2.65 us (2%)
    all_gather x1, blocking collectives, local(): table = lax.all_gather(green_blocks[0], 'blk', axis=0, tiled=True)  63 us
    dot_general x3, matrix products, contract(): lax.dot_general(first.reshape(-1, width), second.reshape(-1, width), (((0...  27.8 us
    dot_general x3, matrix products, transform(): jnp.einsum('sn,mnb->smb', right, source, preferred_element_type=jnp.float32)  14.1 us
    unnamed x11, local copies, waits for them, and re-layouts  6.92 us
    ppermute x4, waiting for transfers between devices, exchange(): piece = lax.ppermute(piece, ('tau', 'blk'), perm)  6.32 us
    ppermute x1, starting transfers between devices, local(): partner = lax.ppermute(flipped, 'blk', ahead)  5.45 us
    ppermute x4, starting transfers between devices, exchange(): piece = lax.ppermute(piece, ('tau', 'blk'), perm)  3.14 us
  transfers between devices with their start and end apart: 6, of which 3 were waited for; matrix products, arithmetic and copies ran while one was open for 22% of the time, Pallas kernels for 0%

profile of v1, /device:TPU:0, one launch (start us, length us, event | category | flops | bytes accessed | tf_op | source)
XLA Modules:
  0.0 135.0 jit_solution(174023814726196317)
XLA Ops:
  0.0 6.9 %copy.66 = bf16[1,128,128,128]{3,1,2,0:T(8,128)(2,1)} copy(bf16[1,128,128,128]{3,2,1,0:T(8,128)(2,1)} %param.5) | data formatting | bytes 8388608 | tf_op args[0]
  6.9 5.5 %collective-permute-start.1 = (bf16[128,128,128]{2,1,0:T(8,128)(2,1)}, bf16[128,128,128]{2,1,0:T(8,128)(2,1)}, u32[]{:S(2)}, u32[]{:S(2)}) collective-permute-start(bf16[128,128,128]{2,1,0:T(8,128)(2,1)} %bitcast.61), channel_id=1, source_target_pairs={{0,15},{1,0},{2,1},{3,2},{4,3},{5,4},{6,5},{7,6},{8,7},{9,8},{10,9... | collective-permute-start | bytes 12582920 | tf_op jit(solution)/shard_map/ppermute | solution.py:66
  12.4 0.7 collective-permute-start
  13.2 63.0 %all-gather = bf16[1,128,2048]{2,1,0:T(8,128)(2,1)S(1)} all-gather(bf16[1,8,2048]{2,1,0:T(8,128)(2,1)S(1)} %copy-done.1), channel_id=2, replica_groups=mesh['tau'=2,'blk'=16] {'blk'}, dimensions={1}, use_global_device_ids=true | all-gather | bytes 557056 | tf_op jit(solution)/shard_map/all_gather | solution.py:61
  76.2 0.6 constant_dynamic-slice_fusion.1
  76.9 0.7 gather_fusion
  77.6 0.6 reshape.115
  78.1 0.6 copy.67
  78.8 0.4 fusion.31
  79.2 0.1 reshape.131
  79.3 0.1 reshape.129
  79.4 0.1 reshape.128
  79.6 5.4 %fusion.10 = bf16[128,128,128]{2,0,1:T(8,128)(2,1)} fusion(bf16[128,128,1]{1,0,2:T(8,128)(2,1)S(1)} %reshape.128, bf16[1,128,128,128]{3,2,1,0:T(8,128)(2,1)} %param.5), kind=kOutput, calls=%fused_computation.14 | convolution fusion | flops 536870912 | bytes 8421376 | tf_op jit(solution)/shard_map/sn,mnb->smb/dot_general | solution.py:18
  85.0 10.1 %broadcast_multiply_fusion = (f32[128,128]{0,1:T(8,128)S(1)}, f32[128,128]{0,1:T(8,128)S(1)}) fusion(f32[]{:T(128)} %bitcast.12, bf16[128,128,128]{2,0,1:T(8,128)(2,1)} %bitcast.64, bf16[128,128,1]{1,0,2:T(8,128)(2,1)S(1)} %reshape.129, bf16[128,128,128]{2,0,1:T(8,128)(2,1)} %fusion.10), kind=kOutput, calls=%fused_computation.33 | convolution fusion | flops 1075855360 | bytes 8552452 | tf_op jit(solution)/shard_map/dot_general | solution.py:28
  95.0 1.6 %collective-permute-start.4 = (f32[128,128]{0,1:T(8,128)S(1)}, f32[128,128]{0,1:T(8,128)S(1)}, u32[]{:S(2)}, u32[]{:S(2)}) collective-permute-start(f32[128,128]{0,1:T(8,128)S(1)} %get-tuple-element.15), channel_id=1, source_target_pairs={{0,16},{1,17},{2,18},{3,19},{4,20},{5,21},{6,22},{7,23},{8,24},{9,... | collective-permute-start | bytes 196616 | tf_op jit(solution)/shard_map/ppermute | solution.py:50
  96.6 0.1 reshape.125
  96.7 5.5 %fusion.14 = bf16[128,128,128]{2,0,1:T(8,128)(2,1)} fusion(bf16[128,128,1]{1,0,2:T(8,128)(2,1)S(1)} %reshape.131, bf16[1,128,128,128]{3,2,1,0:T(8,128)(2,1)} %param.5), kind=kOutput, calls=%fused_computation.18 | convolution fusion | flops 536870912 | bytes 8421376 | tf_op jit(solution)/shard_map/sn,mnb->smb/dot_general | solution.py:18
  102.3 3.2 %fusion.12 = bf16[128,128,128]{2,0,1:T(8,128)(2,1)} fusion(bf16[128,128,1]{1,0,2:T(8,128)(2,1)S(1)} %reshape.125, bf16[1,128,128,128]{3,2,1,0:T(8,128)(2,1)S(1)} %copy-done), kind=kOutput, calls=%fused_computation.16 | convolution fusion | flops 536870912 | bytes 8421376 | tf_op jit(solution)/shard_map/sn,mnb->smb/dot_general | solution.py:18
  105.5 0.1 reshape.132
  105.6 0.1 reshape.126
  105.8 0.7 multiply_add_fusion.1
  106.4 9.3 %fusion.19 = f32[128,128]{1,0:T(8,128)S(1)} fusion(bf16[128,128,128]{2,1,0:T(8,128)(2,1)} %collective-permute-done.1, bf16[128,128,1]{1,0,2:T(8,128)(2,1)S(1)} %reshape.126, bf16[128,128,128]{2,0,1:T(8,128)(2,1)} %fusion.12), kind=kOutput, calls=%fused_computation.24 | convolution fusion | flops 1075838976 | bytes 8486912 | tf_op jit(solution)/shard_map/dot_general | solution.py:28
  115.8 0.6 multiply_bitcast_fusion
  116.4 8.4 %broadcast_multiply_fusion.1 = (f32[128,128]{0,1:T(8,128)S(1)}, f32[128,128]{0,1:T(8,128)S(1)}) fusion(f32[]{:T(128)} %bitcast.12, bf16[128,128,128]{2,1,0:T(8,128)(2,1)} %collective-permute-done.1, bf16[128,128,1]{1,0,2:T(8,128)(2,1)S(1)} %reshape.132, bf16[128,128,128]{2,0,1:T(8,128)(2,1)} %fusion.14), kind=kOutput, calls=%fused_computation.34 | convolution fusion | flops 1075855360 | bytes 8552452 | tf_op jit(solution)/shard_map/dot_general | solution.py:28
  124.8 0.6 collective-permute-start.5
  125.4 0.7 multiply_bitcast_fusion.1
  126.2 0.9 collective-permute-start.3
  127.1 2.7 %collective-permute-done.5 = f32[128,128]{0,1:T(8,128)S(1)} collective-permute-done((f32[128,128]{0,1:T(8,128)S(1)}, f32[128,128]{0,1:T(8,128)S(1)}, u32[]{:S(2)}, u32[]{:S(2)}) %collective-permute-start.5) | collective-permute-done | bytes 65568 | tf_op jit(solution)/shard_map/ppermute | solution.py:50
  129.7 0.7 multiply_add_fusion
  130.4 2.1 %collective-permute-done.2 = f32[128,128]{1,0:T(8,128)S(1)} collective-permute-done((f32[128,128]{1,0:T(8,128)S(1)}, f32[128,128]{1,0:T(8,128)S(1)}, u32[]{:S(2)}, u32[]{:S(2)}) %collective-permute-start.2) | collective-permute-done | bytes 65568 | tf_op jit(solution)/shard_map/ppermute | solution.py:50
  132.6 1.5 %collective-permute-done.3 = f32[128,128]{0,1:T(8,128)S(1)} collective-permute-done((f32[128,128]{0,1:T(8,128)S(1)}, f32[128,128]{0,1:T(8,128)S(1)}, u32[]{:S(2)}, u32[]{:S(2)}) %collective-permute-start.3) | collective-permute-done | bytes 65568 | tf_op jit(solution)/shard_map/ppermute | solution.py:50
  134.2 0.8 copy.20
  (23 shorter events, 0.4 us)
Async XLA Ops:
  0.0 12.4 %copy-start.2 = (s32[48]{0:T(128)S(1)}, s32[48]{0:T(128)}, u32[]{:S(2)}) copy-start(s32[48]{0:T(128)} %param.8) | copy-start | bytes 580
  0.0 12.4 %copy-start.3 = (s32[48]{0:T(128)S(1)}, s32[48]{0:T(128)}, u32[]{:S(2)}) copy-start(s32[48]{0:T(128)} %param.7) | copy-start | bytes 580
  0.0 13.2 %copy-start.4 = (f32[2,1]{0,1:T(1,128)S(1)}, f32[2,1]{0,1:T(1,128)}, u32[]{:S(2)}) copy-start(f32[2,1]{0,1:T(1,128)} %param.9) | copy-start | bytes 28
  0.0 13.2 %copy-start.1 = (bf16[1,8,2048]{2,1,0:T(8,128)(2,1)S(1)}, bf16[1,8,2048]{2,1,0:T(8,128)(2,1)}, u32[]{:S(2)}) copy-start(bf16[1,8,2048]{2,1,0:T(8,128)(2,1)} %param.6) | copy-start | bytes 98308
  6.9 99.5 %collective-permute-start.1 = (bf16[128,128,128]{2,1,0:T(8,128)(2,1)}, bf16[128,128,128]{2,1,0:T(8,128)(2,1)}, u32[]{:S(2)}, u32[]{:S(2)}) collective-permute-start(bf16[128,128,128]{2,1,0:T(8,128)(2,1)} %bitcast.61), channel_id=1, source_target_pairs={{0,15},{1,0},{2,1},{3,2},{4,3},{5,4},{6,5},{7,6},{8,7},{9,8},{10,9... | collective-permute-start | bytes 12582920 | tf_op jit(solution)/shard_map/ppermute | solution.py:66
  12.4 64.4 %collective-permute-start = (s32[16]{0:T(128)S(1)}, s32[16]{0:T(128)S(1)}, u32[]{:S(2)}, u32[]{:S(2)}) collective-permute-start(s32[16]{0:T(128)S(1)} %bitcast.68), channel_id=1, source_target_pairs={{0,15},{1,0},{2,1},{3,2},{4,3},{5,4},{6,5},{7,6},{8,7},{9,8},{10,9... | collective-permute-start | bytes 200 | tf_op jit(solution)/shard_map/ppermute | solution.py:62
  95.0 10.7 %collective-permute-start.4 = (f32[128,128]{0,1:T(8,128)S(1)}, f32[128,128]{0,1:T(8,128)S(1)}, u32[]{:S(2)}, u32[]{:S(2)}) collective-permute-start(f32[128,128]{0,1:T(8,128)S(1)} %get-tuple-element.15), channel_id=1, source_target_pairs={{0,16},{1,17},{2,18},{3,19},{4,20},{5,21},{6,22},{7,23},{8,24},{9,... | collective-permute-start | bytes 196616 | tf_op jit(solution)/shard_map/ppermute | solution.py:50
  96.7 5.6 %copy-start = (bf16[1,128,128,128]{3,2,1,0:T(8,128)(2,1)S(1)}, bf16[1,128,128,128]{3,2,1,0:T(8,128)(2,1)}, u32[]{:S(2)}) copy-start(bf16[1,128,128,128]{3,2,1,0:T(8,128)(2,1)} %param.5) | copy-start | bytes 12582916
  124.8 4.9 %collective-permute-start.5 = (f32[128,128]{0,1:T(8,128)S(1)}, f32[128,128]{0,1:T(8,128)S(1)}, u32[]{:S(2)}, u32[]{:S(2)}) collective-permute-start(f32[128,128]{0,1:T(8,128)S(1)} %get-tuple-element.13), channel_id=1, source_target_pairs={{0,16},{1,17},{2,18},{3,19},{4,20},{5,21},{6,22},{7,23},{8,24},{9,... | collective-permute-start | bytes 196616 | tf_op jit(solution)/shard_map/ppermute | solution.py:50
  126.1 6.4 %collective-permute-start.2 = (f32[128,128]{1,0:T(8,128)S(1)}, f32[128,128]{1,0:T(8,128)S(1)}, u32[]{:S(2)}, u32[]{:S(2)}) collective-permute-start(f32[128,128]{1,0:T(8,128)S(1)} %multiply_bitcast_fusion.1), channel_id=1, source_target_pairs={{0,1},{1,2},{2,3},{3,4},{4,5},{5,6},{6,7},{7,8},{8,9},{9,10},{10,1... | collective-permute-start | bytes 196616 | tf_op jit(solution)/shard_map/ppermute | solution.py:50
  126.2 8.0 %collective-permute-start.3 = (f32[128,128]{0,1:T(8,128)S(1)}, f32[128,128]{0,1:T(8,128)S(1)}, u32[]{:S(2)}, u32[]{:S(2)}) collective-permute-start(f32[128,128]{0,1:T(8,128)S(1)} %multiply_bitcast_fusion), channel_id=1, source_target_pairs={{0,17},{1,18},{2,19},{3,20},{4,21},{5,22},{6,23},{7,24},{8,25},{9,... | collective-permute-start | bytes 196616 | tf_op jit(solution)/shard_map/ppermute | solution.py:50

commit v2 on v1

--- a/solution.py
+++ b/solution.py
@@ -5,7 +5,7 @@
 
 AB = 32
 NS = 4
-HALF = 1
+CHUNKS = 2
 
 
 def green_pairs(blocks):
@@ -52,26 +52,59 @@
     return total
 
 
+def pull_ahead(value):
+    taus = lax.axis_size("tau")
+    blks = lax.axis_size("blk")
+    rows = value.shape[0]
+    if taus != 2 or blks % 2 or rows % (2 * CHUNKS):
+        whole = lax.ppermute(value, "blk", [(i, (i - 1) % blks) for i in range(blks)])
+        return [(0, whole)]
+    t = lax.axis_index("tau")
+    odd = lax.axis_index("blk") % 2 == 1
+    half = rows // 2
+    step = half // CHUNKS
+    mine, other = t * half, (1 - t) * half
+    evens = [(i, (i - 1) % blks) for i in range(0, blks, 2)]
+    odds = [(i, i - 1) for i in range(1, blks, 2)]
+    swap = [(i * blks + j, (1 - i) * blks + j) for i in range(2) for j in range(1, blks, 2)]
+    near, far = [], []
+    for k in range(CHUNKS):
+        part = lax.dynamic_slice_in_dim(value, mine + k * step, step, 0)
+        near.append(lax.ppermute(part, "blk", evens))
+    whole = lax.ppermute(value, "blk", odds)
+    for part in near:
+        far.append(lax.ppermute(part, ("tau", "blk"), swap))
+    first = jnp.where(odd, jnp.concatenate(near), lax.dynamic_slice_in_dim(whole, mine, half, 0))
+    second = jnp.where(odd, jnp.concatenate(far), lax.dynamic_slice_in_dim(whole, other, half, 0))
+    return [(mine, first), (other, second)]
+
+
 def local(three_center, green_blocks, block_owner, block_slot, fold_weights):
     source = three_center[0]
     devices = lax.axis_size("blk")
     per_slot = NS * NS
-    ahead = [(i, (i - 1) % devices) for i in range(devices)]
     ids = block_owner * green_blocks.shape[1] + block_slot
+    next_ids = lax.ppermute(ids[:per_slot], "blk", [(i, (i - 1) % devices) for i in range(devices)])
     table = lax.all_gather(green_blocks[0], "blk", axis=0, tiled=True)
-    next_ids = lax.ppermute(ids[:per_slot], "blk", ahead)
     used = jnp.concatenate([next_ids, ids[per_slot:]])
+    flipped = source.transpose(1, 0, 2)
+    table, used, sent = lax.optimization_barrier((table, used, flipped))
+    halves = pull_ahead(sent)
     fetched = table.at[used].get(mode="promise_in_bounds")
-    flipped = source.transpose(1, 0, 2)
-    partner = lax.ppermute(flipped, "blk", ahead)
     occupied, virtual = green_pairs(fetched)
     weights = fold_weights[:, 0] * -2.0
     own = transform(occupied[1], virtual[1], source)
+    out_own = exchange(contract(own, flipped), weights, 0)
     down = transform(occupied[0].T, virtual[0].T, source)
     up = transform(occupied[2], virtual[2], source)
-    out_own = exchange(contract(own, flipped), weights, 0)
-    out_down = exchange(contract(partner, down), weights, 1)
-    out_up = exchange(contract(up, partner), weights, 0)
+    down, up = lax.optimization_barrier((down, up))
+    chi_down = chi_up = 0.0
+    for start, half in halves:
+        rows = half.shape[0]
+        chi_down += contract(half, lax.dynamic_slice_in_dim(down, start, rows, 0))
+        chi_up += contract(lax.dynamic_slice_in_dim(up, start, rows, 0), half)
+    out_down = exchange(chi_down, weights, 1)
+    out_up = exchange(chi_up, weights, 0)
     return jnp.concatenate([out_down, out_own, out_up], axis=1)[None]
 
 

time: 135 us -> 129 us (0.956)
  blocking collectives: 63 us -> 19.3 us
  local copies, waits for them, and re-layouts: 11.6 us -> 31.6 us
  starting transfers between devices: 9.33 us -> 22.3 us
  other arithmetic: 2.65 us -> 7.52 us
    all_gather x1, blocking collectives: 63 us -> 19.3 us  [local(): table = lax.all_gather(green_blocks[0], 'blk', axis=0, tiled=True)]
    dynamic_slice x0 -> x4, local copies, waits for them, and re-layouts: none -> 13.9 us  [the longest x3 11 us: local(): chi_down += contract(half, lax.dynamic_slice_in_dim(down, start, rows, 0))]
    dot_general x1 -> x2, local copies, waits for them, and re-layouts: 0.09 us -> 13.8 us  [transform(): jnp.einsum('sn,mnb->smb', right, source, preferred_element_type=jnp.float32)]
    ppermute x2 -> x6, starting transfers between devices: 6.18 us -> 18.5 us  [the longest x2 8.49 us: pull_ahead(): near.append(lax.ppermute(part, 'blk', evens))]
    dot_general x3 -> x5, matrix products: 27.8 us -> 17 us  [contract(): lax.dot_general(first.reshape(-1, width), second.reshape(-1, width), (((0...]
    dot_general x0 -> x2, matrix products: none -> 8.63 us  [transform(): jnp.einsum('lm,smb->slb', left, halfway, preferred_element_type=jnp.float32)]
    unnamed x11 -> x8, local copies, waits for them, and re-layouts: 6.92 us -> 0.26 us
    select_n x0 -> x1, other arithmetic: none -> 4.09 us  [pull_ahead(): jnp.where(odd, jnp.concatenate(far), lax.dynamic_slice_in_dim(whole, othe...]
  transfers between devices with their start and end apart: 6 -> 10, of which waited for: 3 -> 2; matrix products, arithmetic and copies ran while one was open for 22% -> 56% of each run, Pallas kernels for 0% -> 0%
where the time goes in v2:
time: 129 us
  matrix products  42 us (33%)
  local copies, waits for them, and re-layouts  31.6 us (24%)
  starting transfers between devices  22.3 us (17%)
  blocking collectives  19.3 us (15%)
  other arithmetic  7.52 us (6%)
  waiting for transfers between devices  5.72 us (4%)
    all_gather x1, blocking collectives, local(): table = lax.all_gather(green_blocks[0], 'blk', axis=0, tiled=True)  19.3 us
    dot_general x5, matrix products, contract(): lax.dot_general(first.reshape(-1, width), second.reshape(-1, width), (((0...  17 us
    dot_general x3, matrix products, transform(): jnp.einsum('sn,mnb->smb', right, source, preferred_element_type=jnp.float32)  16.4 us
    dot_general x2, local copies, waits for them, and re-layouts, transform(): jnp.einsum('sn,mnb->smb', right, source, preferred_element_type=jnp.float32)  13.8 us
    dynamic_slice x3, local copies, waits for them, and re-layouts, local(): chi_down += contract(half, lax.dynamic_slice_in_dim(down, start, rows, 0))  11 us
    dot_general x2, matrix products, transform(): jnp.einsum('lm,smb->slb', left, halfway, preferred_element_type=jnp.float32)  8.63 us
    ppermute x2, starting transfers between devices, pull_ahead(): near.append(lax.ppermute(part, 'blk', evens))  8.49 us
    ppermute x4, waiting for transfers between devices, exchange(): piece = lax.ppermute(piece, ('tau', 'blk'), perm)  5.7 us
  transfers between devices with their start and end apart: 10, of which 2 were waited for; matrix products, arithmetic and copies ran while one was open for 56% of the time, Pallas kernels for 0%

profile of v2, /device:TPU:0, one launch (start us, length us, event | category | flops | bytes accessed | tf_op | source)
XLA Modules:
  0.0 128.7 jit_solution(90928163966543395)
XLA Ops:
  0.0 0.7 multiply_add_fusion.2
  0.7 5.4 %collective-permute-start = (s32[16]{0:T(128)S(1)}, s32[16]{0:T(128)S(1)}, u32[]{:S(2)}, u32[]{:S(2)}) collective-permute-start(s32[16]{0:T(128)S(1)} %bitcast.62), channel_id=1, source_target_pairs={{0,15},{1,0},{2,1},{3,2},{4,3},{5,4},{6,5},{7,6},{8,7},{9,8},{10,9... | collective-permute-start | bytes 200 | tf_op jit(solution)/shard_map/ppermute | solution.py:87
  6.2 19.3 %all-gather = bf16[1,128,2048]{2,1,0:T(8,128)(2,1)S(1)} all-gather(bf16[1,8,2048]{2,1,0:T(8,128)(2,1)} %param.6), channel_id=2, replica_groups=mesh['tau'=2,'blk'=16] {'blk'}, dimensions={1}, use_global_device_ids=true | all-gather | bytes 557056 | tf_op jit(solution)/shard_map/all_gather | solution.py:88
  25.6 1.3 collective-permute-start.3
  26.9 0.7 broadcast_multiply_fusion.4
  28.1 2.9 %constant_dynamic-slice_fusion.4 = (bf16[32,128,128]{2,0,1:T(8,128)(2,1)S(1)}, bf16[32,128,128]{2,0,1:T(8,128)(2,1)}) fusion(bf16[128,128,128]{2,0,1:T(8,128)(2,1)} %bitcast.58, s32[]{:T(128)S(6)} %select_n.50, s32[]{:T(128)S(6)} %select_n.51), kind=kLoop, calls=%fused_computation.50 | loop fusion | bytes 4194312 | tf_op jit(solution)/shard_map/dynamic_slice | solution.py:72
  31.0 6.2 %collective-permute-start.2 = (bf16[32,128,128]{2,0,1:T(8,128)(2,1)}, bf16[32,128,128]{2,0,1:T(8,128)(2,1)S(1)}, u32[]{:S(2)}, u32[]{:S(2)}) collective-permute-start(bf16[32,128,128]{2,0,1:T(8,128)(2,1)} %get-tuple-element.20), channel_id=1, source_target_pairs={{0,15},{2,1},{4,3},{6,5},{8,7},{10,9},{12,11},{14,13},{16,31},{18,... | collective-permute-start | bytes 3145736 | tf_op jit(solution)/shard_map/ppermute | solution.py:73
  37.3 2.3 %collective-permute-start.1 = (bf16[32,128,128]{2,0,1:T(8,128)(2,1)S(1)}, bf16[32,128,128]{2,0,1:T(8,128)(2,1)}, u32[]{:S(2)}, u32[]{:S(2)}) collective-permute-start(bf16[32,128,128]{2,0,1:T(8,128)(2,1)S(1)} %get-tuple-element.19), channel_id=1, source_target_pairs={{0,15},{2,1},{4,3},{6,5},{8,7},{10,9},{12,11},{14,13},{16,31},{18,... | collective-permute-start | bytes 3145736 | tf_op jit(solution)/shard_map/ppermute | solution.py:73
  39.5 0.7 gather_fusion
  42.1 5.5 %fusion.5 = bf16[128,128,128]{2,0,1:T(8,128)(2,1)} fusion(bf16[128,128,1]{1,0,2:T(8,128)(2,1)S(1)} %reshape.47, bf16[1,128,128,128]{3,2,1,0:T(8,128)(2,1)} %param.5), kind=kOutput, calls=%fused_computation.7 | convolution fusion | flops 536870912 | bytes 8421376 | tf_op jit(solution)/shard_map/sn,mnb->smb/dot_general | solution.py:18
  47.6 6.9 %copy.20 = bf16[128,128,128]{1,2,0:T(8,128)(2,1)} copy(bf16[128,128,128]{2,0,1:T(8,128)(2,1)} %fusion.5) | data formatting | bytes 8388608 | tf_op jit(solution)/shard_map/sn,mnb->smb/dot_general | solution.py:18
  54.6 5.6 %fusion.3 = bf16[128,128,128]{2,0,1:T(8,128)(2,1)} fusion(bf16[128,128,1]{1,0,2:T(8,128)(2,1)S(1)} %reshape.49, bf16[1,128,128,128]{3,2,1,0:T(8,128)(2,1)} %param.5), kind=kOutput, calls=%fused_computation.5 | convolution fusion | flops 536870912 | bytes 8421376 | tf_op jit(solution)/shard_map/sn,mnb->smb/dot_general | solution.py:18
  60.2 3.2 %convert_bitcast_fusion.1 = bf16[128,128,128]{1,2,0:T(8,128)(2,1)} fusion(bf16[128,128,1]{1,0,2:T(8,128)(2,1)S(1)} %reshape.48, bf16[128,128,128]{1,2,0:T(8,128)(2,1)S(1)} %copy-done), kind=kOutput, calls=%fused_computation.16 | convolution fusion | flops 538968064 | bytes 8421376 | tf_op jit(solution)/shard_map/lm,smb->slb/dot_general | solution.py:21
  63.5 6.9 %copy.21 = bf16[128,128,128]{1,2,0:T(8,128)(2,1)} copy(bf16[128,128,128]{2,0,1:T(8,128)(2,1)} %fusion.3) | data formatting | bytes 8388608 | tf_op jit(solution)/shard_map/sn,mnb->smb/dot_general | solution.py:18
  70.4 5.4 %convert_bitcast_fusion = bf16[128,128,128]{1,2,0:T(8,128)(2,1)} fusion(bf16[128,128,1]{1,0,2:T(8,128)(2,1)S(1)} %reshape.50, bf16[128,128,128]{1,2,0:T(8,128)(2,1)} %copy.21), kind=kOutput, calls=%fused_computation.13 | convolution fusion | flops 538968064 | bytes 8421376 | tf_op jit(solution)/shard_map/lm,smb->slb/dot_general | solution.py:21
  76.1 5.4 %fusion.7 = bf16[128,128,128]{2,0,1:T(8,128)(2,1)} fusion(bf16[128,128,1]{1,0,2:T(8,128)(2,1)S(1)} %reshape.53, bf16[1,128,128,128]{3,2,1,0:T(8,128)(2,1)} %param.5), kind=kOutput, calls=%fused_computation.9 | convolution fusion | flops 536870912 | bytes 8421376 | tf_op jit(solution)/shard_map/sn,mnb->smb/dot_general | solution.py:18
  81.5 1.6 %collective-permute-start.5 = (bf16[32,128,128]{2,0,1:T(8,128)(2,1)S(1)}, bf16[32,128,128]{2,0,1:T(8,128)(2,1)}, u32[]{:S(2)}, u32[]{:S(2)}) collective-permute-start(bf16[32,128,128]{2,0,1:T(8,128)(2,1)S(1)} %collective-permute-done.2), channel_id=1, source_target_pairs={{1,17},{3,19},{5,21},{7,23},{9,25},{11,27},{13,29},{15,31},{17,1},... | collective-permute-start | bytes 3145736 | tf_op jit(solution)/shard_map/ppermute | solution.py:76
  83.1 1.6 %collective-permute-start.4 = (bf16[32,128,128]{2,0,1:T(8,128)(2,1)}, bf16[32,128,128]{2,0,1:T(8,128)(2,1)}, u32[]{:S(2)}, u32[]{:S(2)}) collective-permute-start(bf16[32,128,128]{2,0,1:T(8,128)(2,1)} %collective-permute-done.1), channel_id=1, source_target_pairs={{1,17},{3,19},{5,21},{7,23},{9,25},{11,27},{13,29},{15,31},{17,1},... | collective-permute-start | bytes 3145736 | tf_op jit(solution)/shard_map/ppermute | solution.py:76
  84.7 10.4 %broadcast_multiply_fusion.1 = (f32[128,128]{1,0:T(8,128)S(1)}, f32[128,128]{1,0:T(8,128)S(1)}) fusion(f32[]{:T(128)} %bitcast.9, bf16[128,128,128]{2,0,1:T(8,128)(2,1)} %bitcast.59, bf16[128,128,1]{1,0,2:T(8,128)(2,1)S(1)} %reshape.54, bf16[128,128,128]{2,0,1:T(8,128)(2,1)} %fusion.7), kind=kOutput, calls=%fused_computation.39 | convolution fusion | flops 1075855360 | bytes 8552452 | tf_op jit(solution)/shard_map/dot_general | solution.py:28
  95.1 1.6 %collective-permute-start.8 = (f32[128,128]{1,0:T(8,128)S(1)}, f32[128,128]{1,0:T(8,128)S(1)}, u32[]{:S(2)}, u32[]{:S(2)}) collective-permute-start(f32[128,128]{1,0:T(8,128)S(1)} %get-tuple-element.33), channel_id=1, source_target_pairs={{0,16},{1,17},{2,18},{3,19},{4,20},{5,21},{6,22},{7,23},{8,24},{9,... | collective-permute-start | bytes 196616 | tf_op jit(solution)/shard_map/ppermute | solution.py:50
  96.7 4.0 %constant_dynamic-slice_fusion.1 = (bf16[64,128,128]{1,2,0:T(8,128)(2,1)S(1)}, bf16[64,128,128]{1,2,0:T(8,128)(2,1)}) fusion(bf16[128,128,128]{1,2,0:T(8,128)(2,1)} %convert_bitcast_fusion.1, s32[]{:T(128)S(6)} %select_n.54, s32[]{:T(128)S(6)} %select_n.50), kind=kLoop, calls=%fused_computation.47 | loop fusion | bytes 8388616 | tf_op jit(solution)/shard_map/dynamic_slice | solution.py:104
  100.7 4.2 %copy.23 = bf16[64,128,128]{2,0,1:T(8,128)(2,1)} copy(bf16[64,128,128]{1,2,0:T(8,128)(2,1)} %get-tuple-element.16) | data formatting | bytes 4194304 | tf_op jit(solution)/shard_map/dynamic_slice | solution.py:104
  104.9 2.8 %copy.25 = bf16[64,128,128]{2,0,1:T(8,128)(2,1)} copy(bf16[64,128,128]{1,2,0:T(8,128)(2,1)S(1)} %get-tuple-element.15) | data formatting | bytes 4194304 | tf_op jit(solution)/shard_map/dynamic_slice | solution.py:104
  108.4 4.1 %maximum_select_fusion.1 = (bf16[64,128,128]{2,0,1:T(8,128)(2,1)S(1)}, bf16[64,128,128]{2,0,1:T(8,128)(2,1)S(1)}) fusion(bf16[32,128,128]{2,0,1:T(8,128)(2,1)} %collective-permute-done.5, bf16[32,128,128]{2,0,1:T(8,128)(2,1)} %collective-permute-done.4, bf16[128,128,128]{2,0,1:T(8,128)(2,1)} %collective-permute-done.3, s32[]{:T(128)S(6)} %select_n.54, ...), kind=kLoop, calls=%fused_computation.20 | loop fusion | flops 10485760 | bytes 12582921 | tf_op jit(solution)/shard_map/jit(_where)/select_n | solution.py:78
  112.7 1.5 %fusion.25 = f32[128,128]{1,0:T(8,128)S(1)} fusion(bf16[64,128,128]{2,0,1:T(8,128)(2,1)S(1)} %get-tuple-element.18, bf16[128,128,128]{1,2,0:T(8,128)(2,1)S(1)} %copy-done.1, s32[]{:T(128)S(6)} %select_n.50), kind=kOutput, calls=%fused_computation.27 | convolution fusion | flops 268435456 | bytes 4259844 | tf_op jit(solution)/shard_map/dot_general | solution.py:28
  114.2 2.3 %broadcast_multiply_fusion = (f32[128,128]{1,0:T(8,128)S(1)}, f32[128,128]{1,0:T(8,128)S(1)}) fusion(f32[]{:T(128)} %bitcast.9, f32[128,128]{1,0:T(8,128)S(1)} %fusion.25, bf16[64,128,128]{2,0,1:T(8,128)(2,1)S(1)} %get-tuple-element.17, bf16[128,128,128]{1,2,0:T(8,128)(2,1)S(1)} %copy-done.1, s32[]{:T(128)S(6)} %select_n.54), kind=kOutput, calls=%fused_computation.38 | convolution fusion | flops 268468224 | bytes 4390920 | tf_op jit(solution)/shard_map/dot_general | solution.py:28
  117.1 0.8 convolution_bitcast_fusion.1
  117.9 2.1 %broadcast_multiply_fusion.2 = (f32[128,128]{1,0:T(8,128)S(1)}, f32[128,128]{1,0:T(8,128)S(1)}) fusion(f32[]{:T(128)} %bitcast.9, f32[]{:T(128)} %bitcast, f32[128,128]{1,0:T(8,128)S(1)} %convolution_bitcast_fusion.1, bf16[64,128,128]{2,0,1:T(8,128)(2,1)S(1)} %get-tuple-element.17, bf16[64,128,128]{2,0,1:T(8,128)(2,1)S(1)} %copy-done.2), kind=kOutput, calls=%fused_computation.40 | convolution fusion | flops 268484608 | bytes 4390920 | tf_op jit(solution)/shard_map/dot_general | solution.py:28
  120.0 1.6 %collective-permute-start.7 = (f32[128,128]{1,0:T(8,128)S(1)}, f32[128,128]{1,0:T(8,128)S(1)}, u32[]{:S(2)}, u32[]{:S(2)}) collective-permute-start(f32[128,128]{1,0:T(8,128)S(1)} %get-tuple-element.27), channel_id=1, source_target_pairs={{0,17},{1,18},{2,19},{3,20},{4,21},{5,22},{6,23},{7,24},{8,25},{9,... | collective-permute-start | bytes 196616 | tf_op jit(solution)/shard_map/ppermute | solution.py:50
  122.3 4.1 %collective-permute-done.6 = f32[128,128]{1,0:T(8,128)S(1)} collective-permute-done((f32[128,128]{1,0:T(8,128)S(1)}, f32[128,128]{1,0:T(8,128)S(1)}, u32[]{:S(2)}, u32[]{:S(2)}) %collective-permute-start.6) | collective-permute-done | bytes 65568 | tf_op jit(solution)/shard_map/ppermute | solution.py:50
  126.4 1.6 %collective-permute-done.7 = f32[128,128]{1,0:T(8,128)S(1)} collective-permute-done((f32[128,128]{1,0:T(8,128)S(1)}, f32[128,128]{1,0:T(8,128)S(1)}, u32[]{:S(2)}, u32[]{:S(2)}) %collective-permute-start.7) | collective-permute-done | bytes 65568 | tf_op jit(solution)/shard_map/ppermute | solution.py:50
  128.0 0.7 maximum_bitcast_fusion
  (35 shorter events, 5.3 us)
Async XLA Ops:
  0.7 24.8 %collective-permute-start = (s32[16]{0:T(128)S(1)}, s32[16]{0:T(128)S(1)}, u32[]{:S(2)}, u32[]{:S(2)}) collective-permute-start(s32[16]{0:T(128)S(1)} %bitcast.62), channel_id=1, source_target_pairs={{0,15},{1,0},{2,1},{3,2},{4,3},{5,4},{6,5},{7,6},{8,7},{9,8},{10,9... | collective-permute-start | bytes 200 | tf_op jit(solution)/shard_map/ppermute | solution.py:87
  25.6 82.8 %collective-permute-start.3 = (bf16[128,128,128]{2,0,1:T(8,128)(2,1)}, bf16[128,128,128]{2,0,1:T(8,128)(2,1)}, u32[]{:S(2)}, u32[]{:S(2)}) collective-permute-start(bf16[128,128,128]{2,0,1:T(8,128)(2,1)} %bitcast.57), channel_id=1, source_target_pairs={{1,0},{3,2},{5,4},{7,6},{9,8},{11,10},{13,12},{15,14},{17,16},{19,... | collective-permute-start | bytes 12582920 | tf_op jit(solution)/shard_map/ppermute | solution.py:74
  31.0 50.4 %collective-permute-start.2 = (bf16[32,128,128]{2,0,1:T(8,128)(2,1)}, bf16[32,128,128]{2,0,1:T(8,128)(2,1)S(1)}, u32[]{:S(2)}, u32[]{:S(2)}) collective-permute-start(bf16[32,128,128]{2,0,1:T(8,128)(2,1)} %get-tuple-element.20), channel_id=1, source_target_pairs={{0,15},{2,1},{4,3},{6,5},{8,7},{10,9},{12,11},{14,13},{16,31},{18,... | collective-permute-start | bytes 3145736 | tf_op jit(solution)/shard_map/ppermute | solution.py:73
  37.3 45.8 %collective-permute-start.1 = (bf16[32,128,128]{2,0,1:T(8,128)(2,1)S(1)}, bf16[32,128,128]{2,0,1:T(8,128)(2,1)}, u32[]{:S(2)}, u32[]{:S(2)}) collective-permute-start(bf16[32,128,128]{2,0,1:T(8,128)(2,1)S(1)} %get-tuple-element.19), channel_id=1, source_target_pairs={{0,15},{2,1},{4,3},{6,5},{8,7},{10,9},{12,11},{14,13},{16,31},{18,... | collective-permute-start | bytes 3145736 | tf_op jit(solution)/shard_map/ppermute | solution.py:73
  54.6 5.6 %copy-start = (bf16[128,128,128]{1,2,0:T(8,128)(2,1)S(1)}, bf16[128,128,128]{1,2,0:T(8,128)(2,1)}, u32[]{:S(2)}) copy-start(bf16[128,128,128]{1,2,0:T(8,128)(2,1)} %copy.20) | copy-start | bytes 12582916
  81.5 26.9 %collective-permute-start.5 = (bf16[32,128,128]{2,0,1:T(8,128)(2,1)S(1)}, bf16[32,128,128]{2,0,1:T(8,128)(2,1)}, u32[]{:S(2)}, u32[]{:S(2)}) collective-permute-start(bf16[32,128,128]{2,0,1:T(8,128)(2,1)S(1)} %collective-permute-done.2), channel_id=1, source_target_pairs={{1,17},{3,19},{5,21},{7,23},{9,25},{11,27},{13,29},{15,31},{17,1},... | collective-permute-start | bytes 3145736 | tf_op jit(solution)/shard_map/ppermute | solution.py:76
  83.1 25.3 %collective-permute-start.4 = (bf16[32,128,128]{2,0,1:T(8,128)(2,1)}, bf16[32,128,128]{2,0,1:T(8,128)(2,1)}, u32[]{:S(2)}, u32[]{:S(2)}) collective-permute-start(bf16[32,128,128]{2,0,1:T(8,128)(2,1)} %collective-permute-done.1), channel_id=1, source_target_pairs={{1,17},{3,19},{5,21},{7,23},{9,25},{11,27},{13,29},{15,31},{17,1},... | collective-permute-start | bytes 3145736 | tf_op jit(solution)/shard_map/ppermute | solution.py:76
  95.1 12.5 %collective-permute-start.8 = (f32[128,128]{1,0:T(8,128)S(1)}, f32[128,128]{1,0:T(8,128)S(1)}, u32[]{:S(2)}, u32[]{:S(2)}) collective-permute-start(f32[128,128]{1,0:T(8,128)S(1)} %get-tuple-element.33), channel_id=1, source_target_pairs={{0,16},{1,17},{2,18},{3,19},{4,20},{5,21},{6,22},{7,23},{8,24},{9,... | collective-permute-start | bytes 196616 | tf_op jit(solution)/shard_map/ppermute | solution.py:50
  108.3 4.4 %copy-start.1 = (bf16[128,128,128]{1,2,0:T(8,128)(2,1)S(1)}, bf16[128,128,128]{1,2,0:T(8,128)(2,1)}, u32[]{:S(2)}) copy-start(bf16[128,128,128]{1,2,0:T(8,128)(2,1)} %convert_bitcast_fusion) | copy-start | bytes 12582916
  112.7 4.4 %copy-start.3 = (bf16[64,128,128]{2,0,1:T(8,128)(2,1)S(1)}, bf16[64,128,128]{2,0,1:T(8,128)(2,1)}, u32[]{:S(2)}) copy-start(bf16[64,128,128]{2,0,1:T(8,128)(2,1)} %copy.23) | copy-start | bytes 6291460
  114.2 3.7 %copy-start.2 = (bf16[64,128,128]{2,0,1:T(8,128)(2,1)S(1)}, bf16[64,128,128]{2,0,1:T(8,128)(2,1)}, u32[]{:S(2)}) copy-start(bf16[64,128,128]{2,0,1:T(8,128)(2,1)} %copy.25) | copy-start | bytes 6291460
  116.5 5.2 %collective-permute-start.9 = (f32[128,128]{1,0:T(8,128)S(1)}, f32[128,128]{1,0:T(8,128)S(1)}, u32[]{:S(2)}, u32[]{:S(2)}) collective-permute-start(f32[128,128]{1,0:T(8,128)S(1)} %get-tuple-element.31), channel_id=1, source_target_pairs={{0,16},{1,17},{2,18},{3,19},{4,20},{5,21},{6,22},{7,23},{8,24},{9,... | collective-permute-start | bytes 196616 | tf_op jit(solution)/shard_map/ppermute | solution.py:50
  119.9 6.4 %collective-permute-start.6 = (f32[128,128]{1,0:T(8,128)S(1)}, f32[128,128]{1,0:T(8,128)S(1)}, u32[]{:S(2)}, u32[]{:S(2)}) collective-permute-start(f32[128,128]{1,0:T(8,128)S(1)} %get-tuple-element.28), channel_id=1, source_target_pairs={{0,1},{1,2},{2,3},{3,4},{4,5},{5,6},{6,7},{7,8},{8,9},{9,10},{10,1... | collective-permute-start | bytes 196616 | tf_op jit(solution)/shard_map/ppermute | solution.py:50
  120.0 8.0 %collective-permute-start.7 = (f32[128,128]{1,0:T(8,128)S(1)}, f32[128,128]{1,0:T(8,128)S(1)}, u32[]{:S(2)}, u32[]{:S(2)}) collective-permute-start(f32[128,128]{1,0:T(8,128)S(1)} %get-tuple-element.27), channel_id=1, source_target_pairs={{0,17},{1,18},{2,19},{3,20},{4,21},{5,22},{6,23},{7,24},{8,25},{9,... | collective-permute-start | bytes 196616 | tf_op jit(solution)/shard_map/ppermute | solution.py:50

commit v3 on v2

v3 whole, which is shorter than its diff:
```python
import functools

import jax
import jax.numpy as jnp
from jax import lax
from jax.experimental import pallas as pl
from jax.experimental.pallas import tpu as pltpu
from jax.sharding import PartitionSpec as P

AB = 32
NS = 4
CHUNKS = 2


def green_pairs(blocks):
    count = blocks.shape[0] // (NS * NS)
    blocks = blocks.reshape(count, NS, NS, 2, AB, AB).transpose(3, 0, 1, 4, 2, 5)
    return blocks.reshape(2, count, NS * AB, NS * AB)


GROUP = 4


def transform_kernel(occupied, virtual, source, own, down, up, flipped, first):
    region = source.shape[0]

    def flip(g, _):
        for k in range(GROUP):
            m = g * GROUP + k
            flipped[pl.ds(m, region, stride=region), :] = source[m].astype(jnp.float32)
        return 0

    lax.fori_loop(0, region // GROUP, flip, 0)

    def left(g, _):
        for k in range(GROUP):
            n = g * GROUP + k
            block = flipped[pl.ds(pl.multiple_of(n * region, region), region), :].astype(jnp.bfloat16)
            product = jnp.dot(occupied[...], block, preferred_element_type=jnp.float32)
            for j in range(3):
                first[j, pl.ds(n, region, stride=region), :] = product[j * region : (j + 1) * region]
        return 0

    lax.fori_loop(0, region // GROUP, left, 0)
    own[...] = jnp.zeros_like(own)

    def right(g, _):
        images = []
        for k in range(GROUP):
            l = g * GROUP + k
            for j, out in enumerate((down, None, up)):
                block = first[j, pl.ds(pl.multiple_of(l * region, region), region), :]
                image = jnp.dot(
                    virtual[j], block.astype(jnp.bfloat16), preferred_element_type=jnp.float32
                ).astype(jnp.bfloat16)
                if out is None:
                    images.append(image)
                else:
                    out[l] = image
        own[...] += lax.dot_general(
            jnp.concatenate(images, axis=0),
            source[pl.ds(g * GROUP, GROUP)].reshape(GROUP * region, -1),
            (((0,), (0,)), ((), ())),
            preferred_element_type=jnp.float32,
        )
        return 0

    lax.fori_loop(0, region // GROUP, right, 0)


def transform(occupied, virtual, source):
    region, _, width = source.shape
    vmem = pl.BlockSpec(memory_space=pltpu.VMEM)
    image = jax.ShapeDtypeStruct((region, region, width), jnp.bfloat16)
    return pl.pallas_call(
        transform_kernel,
        out_shape=(jax.ShapeDtypeStruct((width, width), jnp.float32), image, image),
        in_specs=[vmem] * 3,
        out_specs=(vmem,) * 3,
        scratch_shapes=[
            pltpu.VMEM((region * region, width), jnp.float32),
            pltpu.VMEM((3, region * region, width), jnp.float32),
        ],
        compiler_params=pltpu.CompilerParams(vmem_limit_bytes=56 * 2**20),
        cost_estimate=pl.CostEstimate(
            flops=2 * 7 * region**3 * width, bytes_accessed=12 * 2**20, transcendentals=0
        ),
        name="transform",
    )(occupied.reshape(3 * region, region), virtual, source)


def contract_kernel(pieces, *refs):
    down, up = refs[:2]
    parts = refs[2 : 2 + pieces]
    chi_down, chi_up, held, sem = refs[2 + pieces :]
    region = held.shape[0]

    def bring(source, start):
        copy = pltpu.make_async_copy(source, held.at[pl.ds(start, source.shape[0])], sem)
        copy.start()
        return copy

    if pieces == 1:
        bring(parts[0], 0).wait()
    else:
        t = lax.axis_index("tau")
        odd = lax.axis_index("blk") % 2
        step = parts[1].shape[0]

        @pl.when(odd == 0)
        def _():
            bring(parts[0], 0).wait()

        @pl.when(odd == 1)
        def _():
            for side in range(2):
                start = (t if side == 0 else 1 - t) * (region // 2)
                for k in range(CHUNKS):
                    bring(parts[1 + side * CHUNKS + k], start + k * step).wait()

    chi_down[...] = jnp.zeros_like(chi_down)
    chi_up[...] = jnp.zeros_like(chi_up)
    width = held.shape[2]
    rows = 8

    def body(g, _):
        def flat(ref):
            return ref[pl.ds(g * rows, rows)].reshape(rows * region, width)

        partner = flat(held)
        dims = (((0,), (0,)), ((), ()))
        chi_down[...] += lax.dot_general(partner, flat(down), dims, preferred_element_type=jnp.float32)
        chi_up[...] += lax.dot_general(flat(up), partner, dims, preferred_element_type=jnp.float32)
        return 0

    lax.fori_loop(0, region // rows, body, 0)


def contract(down, up, parts):
    region, _, width = down.shape
    vmem = pl.BlockSpec(memory_space=pltpu.VMEM)
    anywhere = pl.BlockSpec(memory_space=pl.ANY)
    chi = jax.ShapeDtypeStruct((width, width), jnp.float32)
    return pl.pallas_call(
        functools.partial(contract_kernel, len(parts)),
        out_shape=(chi, chi),
        in_specs=[vmem] * 2 + [anywhere] * len(parts),
        out_specs=(vmem, vmem),
        scratch_shapes=[pltpu.VMEM((region, region, width), jnp.bfloat16), pltpu.SemaphoreType.DMA],
        compiler_params=pltpu.CompilerParams(vmem_limit_bytes=32 * 2**20),
        cost_estimate=pl.CostEstimate(
            flops=4 * region**2 * width**2, bytes_accessed=12 * 2**20, transcendentals=0
        ),
        name="contract",
    )(down, up, *parts)


def exchange(chi, weights, step):
    taus = lax.axis_size("tau")
    blks = lax.axis_size("blk")
    t = lax.axis_index("tau")
    total = None
    for shift in range(taus):
        target = lax.rem(t + shift, taus)
        piece = lax.dynamic_index_in_dim(weights, target, 0, keepdims=False) * chi
        if shift or step:
            perm = [
                (i * blks + j, ((i + shift) % taus) * blks + (j + step) % blks)
                for i in range(taus)
                for j in range(blks)
            ]
            piece = lax.ppermute(piece, ("tau", "blk"), perm)
        total = piece if total is None else total + piece
    return total


def pull_ahead(value):
    taus = lax.axis_size("tau")
    blks = lax.axis_size("blk")
    rows = value.shape[0]
    if taus != 2 or blks % 2 or rows % (2 * CHUNKS):
        return [lax.ppermute(value, "blk", [(i, (i - 1) % blks) for i in range(blks)])]
    half = rows // 2
    step = half // CHUNKS
    mine = lax.axis_index("tau") * half
    evens = [(i, (i - 1) % blks) for i in range(0, blks, 2)]
    odds = [(i, i - 1) for i in range(1, blks, 2)]
    swap = [(i * blks + j, (1 - i) * blks + j) for i in range(2) for j in range(1, blks, 2)]
    near, far = [], []
    for k in range(CHUNKS):
        part = lax.dynamic_slice_in_dim(value, mine + k * step, step, 0)
        near.append(lax.ppermute(part, "blk", evens))
    whole = lax.ppermute(value, "blk", odds)
    for part in near:
        far.append(lax.ppermute(part, ("tau", "blk"), swap))
    return [whole, *near, *far]


def local(three_center, green_blocks, block_owner, block_slot, fold_weights):
    source = three_center[0]
    devices = lax.axis_size("blk")
    per_slot = NS * NS
    ids = block_owner * green_blocks.shape[1] + block_slot
    next_ids = lax.ppermute(ids[:per_slot], "blk", [(i, (i - 1) % devices) for i in range(devices)])
    table = lax.all_gather(green_blocks[0], "blk", axis=0, tiled=True)
    used = jnp.concatenate([next_ids, ids[per_slot:]])
    table, used, sent = lax.optimization_barrier((table, used, source))
    parts = pull_ahead(sent)
    fetched = table.at[used].get(mode="promise_in_bounds")
    occupied, virtual = green_pairs(fetched)
    occupied = jnp.concatenate([occupied[:1].swapaxes(1, 2), occupied[1:]])
    virtual = jnp.concatenate([virtual[:1].swapaxes(1, 2), virtual[1:]])
    weights = fold_weights[:, 0] * -2.0
    chi_own, down, up = transform(occupied, virtual, source)
    out_own = exchange(chi_own, weights, 0)
    chi_down, chi_up = contract(down, up, parts)
    out_down = exchange(chi_down, weights, 1)
    out_up = exchange(chi_up, weights, 0)
    return jnp.concatenate([out_down, out_own, out_up], axis=1)[None]


def solution(mesh):
    return jax.shard_map(
        local,
        mesh=mesh,
        in_specs=(
            P("blk", None, None, None),
            P("tau", "blk", None),
            P("blk"),
            P("blk"),
            P(None, "tau"),
        ),
        out_specs=P("tau", "blk", None),
        check_vma=False,
    )
```

time: 129 us -> 144 us (1.12)
  Pallas kernels: 0 us -> 58.6 us
  matrix products: 42 us -> 0 us
  waiting for transfers between devices: 5.72 us -> 24.8 us
  local copies, waits for them, and re-layouts: 31.6 us -> 13.3 us
  starting transfers between devices: 22.3 us -> 19.5 us
    pallas_call x0 -> x2, Pallas kernels: none -> 58.6 us  [the longest x1 50.9 us: transform(): pl.pallas_call(transform_kernel, out_shape=(jax.ShapeDtypeStruct((width,...]
    dot_general x10 -> x0, matrix products: 42 us -> none  [the longest x5 17 us: contract(): lax.dot_general(first.reshape(-1, width), second.reshape(-1, width), (((0...]
    ppermute x2, waiting for transfers between devices: 0.01 us -> 15.9 us  [pull_ahead(): near.append(lax.ppermute(part, 'blk', evens))]
    dot_general x2 -> x0, local copies, waits for them, and re-layouts: 13.8 us -> none  [transform(): jnp.einsum('sn,mnb->smb', right, source, preferred_element_type=jnp.float32)]
    dynamic_slice x3 -> x0, local copies, waits for them, and re-layouts: 11 us -> none  [local(): chi_down += contract(half, lax.dynamic_slice_in_dim(down, start, rows, 0))]
    unnamed x8 -> x6, local copies, waits for them, and re-layouts: 0.26 us -> 4.37 us
    select_n x1 -> x0, other arithmetic: 4.09 us -> none  [pull_ahead(): jnp.where(odd, jnp.concatenate(far), lax.dynamic_slice_in_dim(whole, othe...]
    mul x0 -> x3, other arithmetic: none -> 3.28 us  [exchange(): piece = lax.dynamic_index_in_dim(weights, target, 0, keepdims=False) * chi]
  transfers between devices with their start and end apart: 10 -> 10, of which waited for: 2 -> 6; matrix products, arithmetic and copies ran while one was open for 56% -> 10% of each run, Pallas kernels for 0% -> 35%
where the time goes in v3:
time: 144 us
  Pallas kernels  58.6 us (41%)
  waiting for transfers between devices  24.8 us (17%)
  starting transfers between devices  19.5 us (14%)
  blocking collectives  19.3 us (13%)
  local copies, waits for them, and re-layouts  13.3 us (9%)
  other arithmetic  8.04 us (6%)
    pallas_call x1, Pallas kernels, transform(): pl.pallas_call(transform_kernel, out_shape=(jax.ShapeDtypeStruct((width,...  50.9 us
    all_gather x1, blocking collectives, local(): table = lax.all_gather(green_blocks[0], 'blk', axis=0, tiled=True)  19.3 us
    ppermute x2, waiting for transfers between devices, pull_ahead(): near.append(lax.ppermute(part, 'blk', evens))  15.9 us
    ppermute x4, waiting for transfers between devices, exchange(): piece = lax.ppermute(piece, ('tau', 'blk'), perm)  8.85 us
    pallas_call x1, Pallas kernels, contract(): pl.pallas_call(functools.partial(contract_kernel, len(parts)), out_shape=...  7.69 us
    ppermute x2, starting transfers between devices, pull_ahead(): near.append(lax.ppermute(part, 'blk', evens))  7.57 us
    ppermute x1, starting transfers between devices, local(): lax.ppermute(ids[:per_slot], 'blk', [(i, (i - 1) % devices) for i in rang...  5.44 us
    unnamed x6, local copies, waits for them, and re-layouts  4.37 us
  transfers between devices with their start and end apart: 10, of which 6 were waited for; matrix products, arithmetic and copies ran while one was open for 10% of the time, Pallas kernels for 35%

profile of v3, /device:TPU:0, one launch (start us, length us, event | category | flops | bytes accessed | tf_op | source)
XLA Modules:
  0.0 143.8 jit_solution(17581129454193766378)
XLA Ops:
  0.0 0.7 multiply_add_fusion.2
  0.7 5.4 %collective-permute-start = (s32[16]{0:T(128)S(1)}, s32[16]{0:T(128)S(1)}, u32[]{:S(2)}, u32[]{:S(2)}) collective-permute-start(s32[16]{0:T(128)S(1)} %bitcast.22), channel_id=1, source_target_pairs={{0,15},{1,0},{2,1},{3,2},{4,3},{5,4},{6,5},{7,6},{8,7},{9,8},{10,9... | collective-permute-start | bytes 200 | tf_op jit(solution)/shard_map/ppermute | solution.py:204
  6.1 19.3 %all-gather = bf16[1,128,2048]{2,1,0:T(8,128)(2,1)S(1)} all-gather(bf16[1,8,2048]{2,1,0:T(8,128)(2,1)} %param.6), channel_id=2, replica_groups=mesh['tau'=2,'blk'=16] {'blk'}, dimensions={1}, use_global_device_ids=true | all-gather | bytes 557056 | tf_op jit(solution)/shard_map/all_gather | solution.py:205
  25.6 1.3 collective-permute-start.1
  26.9 3.2 %constant_dynamic-slice_fusion.1 = (bf16[32,128,128]{2,1,0:T(8,128)(2,1)}, bf16[32,128,128]{2,1,0:T(8,128)(2,1)}) fusion(bf16[128,128,128]{2,1,0:T(8,128)(2,1)} %bitcast.17, s32[]{:T(128)S(6)} %select_n.23, s32[]{:T(128)S(6)} %select_n.22), kind=kLoop, calls=%fused_computation.14 | loop fusion | bytes 4194312 | tf_op jit(solution)/shard_map/dynamic_slice | solution.py:191
  30.1 6.2 %collective-permute-start.2 = (bf16[32,128,128]{2,1,0:T(8,128)(2,1)}, bf16[32,128,128]{2,1,0:T(8,128)(2,1)S(1)}, u32[]{:S(2)}, u32[]{:S(2)}) collective-permute-start(bf16[32,128,128]{2,1,0:T(8,128)(2,1)} %get-tuple-element.22), channel_id=1, source_target_pairs={{0,15},{2,1},{4,3},{6,5},{8,7},{10,9},{12,11},{14,13},{16,31},{18,... | collective-permute-start | bytes 3145736 | tf_op jit(solution)/shard_map/ppermute | solution.py:192
  36.3 1.4 collective-permute-start.3
  37.7 0.6 constant_dynamic-slice_fusion.3
  38.3 0.7 gather_fusion
  39.0 1.5 %reshape.21 = bf16[3,4,4,2,32,32]{5,4,3,2,1,0:T(8,128)(2,1)} reshape(bf16[48,2048]{1,0:T(8,128)(2,1)S(1)} %gather_fusion) | data formatting | bytes 393216 | tf_op jit(solution)/shard_map/reshape | solution.py:17
  40.5 1.7 %copy.11 = bf16[3,4,4,2,32,32]{5,2,4,1,0,3:T(4,128)(2,1)S(1)} copy(bf16[3,4,4,2,32,32]{5,4,3,2,1,0:T(8,128)(2,1)} %reshape.21) | data formatting | bytes 393216 | tf_op jit(solution)/shard_map/reshape | solution.py:17
  43.4 5.4 %collective-permute-done.2.refs_3_ = bf16[32,128,128]{2,1,0:T(8,128)(2,1)S(1)} collective-permute-done((bf16[32,128,128]{2,1,0:T(8,128)(2,1)}, bf16[32,128,128]{2,1,0:T(8,128)(2,1)S(1)}, u32[]{:S(2)}, u32[]{:S(2)}) %collective-permute-start.2) | collective-permute-done | bytes 1048608 | tf_op jit(solution)/shard_map/ppermute | solution.py:192
  48.8 0.7 collective-permute-start.4
  49.5 10.5 %collective-permute-done.3.refs_4_ = bf16[32,128,128]{2,1,0:T(8,128)(2,1)S(1)} collective-permute-done((bf16[32,128,128]{2,1,0:T(8,128)(2,1)}, bf16[32,128,128]{2,1,0:T(8,128)(2,1)S(1)}, u32[]{:S(2)}, u32[]{:S(2)}) %collective-permute-start.3) | collective-permute-done | bytes 1048608 | tf_op jit(solution)/shard_map/ppermute | solution.py:192
  60.1 0.7 collective-permute-start.5
  60.8 0.6 pad_maximum_fusion.1.virtual
  61.4 0.7 pad_maximum_fusion
  62.1 50.9 %transform.1 = (f32[128,128]{1,0:T(8,128)}, bf16[128,128,128]{2,1,0:T(8,128)(2,1)}, bf16[128,128,128]{2,1,0:T(8,128)(2,1)}) custom-call(bf16[384,128]{1,0:T(8,128)(2,1)} %bitcast.21, bf16[3,128,128]{2,1,0:T(8,128)(2,1)} %pad_maximum_fusion.1.virtual, bf16[128,128,128]{2,1,0:T(8,128)(2,1)} %bitcast.18), custom_call_target="tpu_custom_call" | custom-call | flops 3758096384 | bytes 12582912 | tf_op jit(solution)/shard_map/transform/pallas_call | solution.py:75
  113.0 1.5 %broadcast_multiply_fusion.1 = f32[128,128]{1,0:T(8,128)S(1)} fusion(f32[128,128]{1,0:T(8,128)} %get-tuple-element.19, f32[]{:T(128)} %bitcast.7), kind=kLoop, calls=%fused_computation.8 | loop fusion | flops 16384 | bytes 131076 | tf_op jit(solution)/shard_map/mul | solution.py:165
  114.5 1.5 %collective-permute-start.8 = (f32[128,128]{1,0:T(8,128)S(1)}, f32[128,128]{1,0:T(8,128)S(1)}, u32[]{:S(2)}, u32[]{:S(2)}) collective-permute-start(f32[128,128]{1,0:T(8,128)S(1)} %broadcast_multiply_fusion.1), channel_id=1, source_target_pairs={{0,16},{1,17},{2,18},{3,19},{4,20},{5,21},{6,22},{7,23},{8,24},{9,... | collective-permute-start | bytes 196616 | tf_op jit(solution)/shard_map/ppermute | solution.py:172
  116.0 2.8 %collective-permute-done.8 = f32[128,128]{1,0:T(8,128)S(1)} collective-permute-done((f32[128,128]{1,0:T(8,128)S(1)}, f32[128,128]{1,0:T(8,128)S(1)}, u32[]{:S(2)}, u32[]{:S(2)}) %collective-permute-start.8) | collective-permute-done | bytes 65568 | tf_op jit(solution)/shard_map/ppermute | solution.py:172
  118.8 1.4 multiply_add_fusion.1
  120.2 2.2 %copy-done = bf16[128,128,128]{2,1,0:T(8,128)(2,1)S(1)} copy-done((bf16[128,128,128]{2,1,0:T(8,128)(2,1)S(1)}, bf16[128,128,128]{2,1,0:T(8,128)(2,1)}, u32[]{:S(2)}) %copy-start) | copy-done | bytes 4194328
  122.4 2.2 %copy-done.1 = bf16[128,128,128]{2,1,0:T(8,128)(2,1)S(1)} copy-done((bf16[128,128,128]{2,1,0:T(8,128)(2,1)S(1)}, bf16[128,128,128]{2,1,0:T(8,128)(2,1)}, u32[]{:S(2)}) %copy-start.1) | copy-done | bytes 4194328
  124.6 7.7 %contract.1 = (f32[128,128]{1,0:T(8,128)S(1)}, f32[128,128]{1,0:T(8,128)S(1)}) custom-call(bf16[128,128,128]{2,1,0:T(8,128)(2,1)S(1)} %copy-done, bf16[128,128,128]{2,1,0:T(8,128)(2,1)S(1)} %copy-done.1, bf16[128,128,128]{2,1,0:T(8,128)(2,1)} %collective-permute-done.1.refs_2_, bf16[32,128,128]{2,1,0:T(8,128)(2,1)S(1)} %collective-permute-done.2.refs_3_, ...), custom_call_target="tpu_custom_call" | custom-call | flops 1073741824 | bytes 12582912 | tf_op jit(solution)/shard_map/contract/pallas_call | solution.py:144
  132.9 1.6 %collective-permute-start.9 = (f32[128,128]{1,0:T(8,128)S(1)}, f32[128,128]{1,0:T(8,128)S(1)}, u32[]{:S(2)}, u32[]{:S(2)}) collective-permute-start(f32[128,128]{1,0:T(8,128)S(1)} %broadcast_multiply_fusion), channel_id=1, source_target_pairs={{0,16},{1,17},{2,18},{3,19},{4,20},{5,21},{6,22},{7,23},{8,24},{9,... | collective-permute-start | bytes 196616 | tf_op jit(solution)/shard_map/ppermute | solution.py:172
  134.5 1.2 broadcast_multiply_fusion.2
  135.7 0.7 collective-permute-start.7
  136.4 0.8 collective-permute-done.9
  137.8 4.3 %collective-permute-done.6 = f32[128,128]{1,0:T(8,128)S(1)} collective-permute-done((f32[128,128]{1,0:T(8,128)S(1)}, f32[128,128]{1,0:T(8,128)S(1)}, u32[]{:S(2)}, u32[]{:S(2)}) %collective-permute-start.6) | collective-permute-done | bytes 65568 | tf_op jit(solution)/shard_map/ppermute | solution.py:172
  142.1 1.0 collective-permute-done.7
  143.1 0.7 maximum_bitcast_fusion
  (25 shorter events, 2.5 us)
Async XLA Ops:
  0.0 37.6 %copy-start.2 = (f32[2,1]{0,1:T(1,128)S(1)}, f32[2,1]{0,1:T(1,128)}, u32[]{:S(2)}) copy-start(f32[2,1]{0,1:T(1,128)} %param.9) | copy-start | bytes 28
  0.7 24.8 %collective-permute-start = (s32[16]{0:T(128)S(1)}, s32[16]{0:T(128)S(1)}, u32[]{:S(2)}, u32[]{:S(2)}) collective-permute-start(s32[16]{0:T(128)S(1)} %bitcast.22), channel_id=1, source_target_pairs={{0,15},{1,0},{2,1},{3,2},{4,3},{5,4},{6,5},{7,6},{8,7},{9,8},{10,9... | collective-permute-start | bytes 200 | tf_op jit(solution)/shard_map/ppermute | solution.py:204
  25.6 94.6 %collective-permute-start.1 = (bf16[128,128,128]{2,1,0:T(8,128)(2,1)}, bf16[128,128,128]{2,1,0:T(8,128)(2,1)}, u32[]{:S(2)}, u32[]{:S(2)}) collective-permute-start(bf16[128,128,128]{2,1,0:T(8,128)(2,1)} %bitcast.16), channel_id=1, source_target_pairs={{1,0},{3,2},{5,4},{7,6},{9,8},{11,10},{13,12},{15,14},{17,16},{19,... | collective-permute-start | bytes 12582920 | tf_op jit(solution)/shard_map/ppermute | solution.py:193
  30.1 18.8 %collective-permute-start.2 = (bf16[32,128,128]{2,1,0:T(8,128)(2,1)}, bf16[32,128,128]{2,1,0:T(8,128)(2,1)S(1)}, u32[]{:S(2)}, u32[]{:S(2)}) collective-permute-start(bf16[32,128,128]{2,1,0:T(8,128)(2,1)} %get-tuple-element.22), channel_id=1, source_target_pairs={{0,15},{2,1},{4,3},{6,5},{8,7},{10,9},{12,11},{14,13},{16,31},{18,... | collective-permute-start | bytes 3145736 | tf_op jit(solution)/shard_map/ppermute | solution.py:192
  36.3 23.8 %collective-permute-start.3 = (bf16[32,128,128]{2,1,0:T(8,128)(2,1)}, bf16[32,128,128]{2,1,0:T(8,128)(2,1)S(1)}, u32[]{:S(2)}, u32[]{:S(2)}) collective-permute-start(bf16[32,128,128]{2,1,0:T(8,128)(2,1)} %get-tuple-element.21), channel_id=1, source_target_pairs={{0,15},{2,1},{4,3},{6,5},{8,7},{10,9},{12,11},{14,13},{16,31},{18,... | collective-permute-start | bytes 3145736 | tf_op jit(solution)/shard_map/ppermute | solution.py:192
  48.8 71.3 %collective-permute-start.4 = (bf16[32,128,128]{2,1,0:T(8,128)(2,1)S(1)}, bf16[32,128,128]{2,1,0:T(8,128)(2,1)S(1)}, u32[]{:S(2)}, u32[]{:S(2)}) collective-permute-start(bf16[32,128,128]{2,1,0:T(8,128)(2,1)S(1)} %collective-permute-done.2.refs_3_), channel_id=1, source_target_pairs={{1,17},{3,19},{5,21},{7,23},{9,25},{11,27},{13,29},{15,31},{17,1},... | collective-permute-start | bytes 3145736 | tf_op jit(solution)/shard_map/ppermute | solution.py:195
  60.1 60.1 %collective-permute-start.5 = (bf16[32,128,128]{2,1,0:T(8,128)(2,1)S(1)}, bf16[32,128,128]{2,1,0:T(8,128)(2,1)S(1)}, u32[]{:S(2)}, u32[]{:S(2)}) collective-permute-start(bf16[32,128,128]{2,1,0:T(8,128)(2,1)S(1)} %collective-permute-done.3.refs_4_), channel_id=1, source_target_pairs={{1,17},{3,19},{5,21},{7,23},{9,25},{11,27},{13,29},{15,31},{17,1},... | collective-permute-start | bytes 3145736 | tf_op jit(solution)/shard_map/ppermute | solution.py:195
  114.5 4.3 %collective-permute-start.8 = (f32[128,128]{1,0:T(8,128)S(1)}, f32[128,128]{1,0:T(8,128)S(1)}, u32[]{:S(2)}, u32[]{:S(2)}) collective-permute-start(f32[128,128]{1,0:T(8,128)S(1)} %broadcast_multiply_fusion.1), channel_id=1, source_target_pairs={{0,16},{1,17},{2,18},{3,19},{4,20},{5,21},{6,22},{7,23},{8,24},{9,... | collective-permute-start | bytes 196616 | tf_op jit(solution)/shard_map/ppermute | solution.py:172
  120.2 2.2 %copy-start = (bf16[128,128,128]{2,1,0:T(8,128)(2,1)S(1)}, bf16[128,128,128]{2,1,0:T(8,128)(2,1)}, u32[]{:S(2)}) copy-start(bf16[128,128,128]{2,1,0:T(8,128)(2,1)} %get-tuple-element.15.refs_0_) | copy-start | bytes 12582916
  122.4 2.2 %copy-start.1 = (bf16[128,128,128]{2,1,0:T(8,128)(2,1)S(1)}, bf16[128,128,128]{2,1,0:T(8,128)(2,1)}, u32[]{:S(2)}) copy-start(bf16[128,128,128]{2,1,0:T(8,128)(2,1)} %get-tuple-element.16.refs_1_) | copy-start | bytes 12582916
  132.9 4.3 %collective-permute-start.9 = (f32[128,128]{1,0:T(8,128)S(1)}, f32[128,128]{1,0:T(8,128)S(1)}, u32[]{:S(2)}, u32[]{:S(2)}) collective-permute-start(f32[128,128]{1,0:T(8,128)S(1)} %broadcast_multiply_fusion), channel_id=1, source_target_pairs={{0,16},{1,17},{2,18},{3,19},{4,20},{5,21},{6,22},{7,23},{8,24},{9,... | collective-permute-start | bytes 196616 | tf_op jit(solution)/shard_map/ppermute | solution.py:172
  135.7 6.4 %collective-permute-start.6 = (f32[128,128]{1,0:T(8,128)S(1)}, f32[128,128]{1,0:T(8,128)S(1)}, u32[]{:S(2)}, u32[]{:S(2)}) collective-permute-start(f32[128,128]{1,0:T(8,128)S(1)} %get-tuple-element.28), channel_id=1, source_target_pairs={{0,1},{1,2},{2,3},{3,4},{4,5},{5,6},{6,7},{7,8},{8,9},{9,10},{10,1... | collective-permute-start | bytes 196616 | tf_op jit(solution)/shard_map/ppermute | solution.py:172
  135.7 7.3 %collective-permute-start.7 = (f32[128,128]{1,0:T(8,128)S(1)}, f32[128,128]{1,0:T(8,128)S(1)}, u32[]{:S(2)}, u32[]{:S(2)}) collective-permute-start(f32[128,128]{1,0:T(8,128)S(1)} %get-tuple-element.27), channel_id=1, source_target_pairs={{0,17},{1,18},{2,19},{3,20},{4,21},{5,22},{6,23},{7,24},{8,25},{9,... | collective-permute-start | bytes 196616 | tf_op jit(solution)/shard_map/ppermute | solution.py:172

commit v4 on v3

v4 whole, which is shorter than its diff:
```python
import functools

import jax
import jax.numpy as jnp
from jax import lax
from jax.experimental import pallas as pl
from jax.experimental.pallas import tpu as pltpu
from jax.sharding import PartitionSpec as P

AB = 32
NS = 4


def green_pairs(blocks):
    count = blocks.shape[0] // (NS * NS)
    blocks = blocks.reshape(count, NS, NS, 2, AB, AB).transpose(3, 0, 1, 4, 2, 5)
    return blocks.reshape(2, count, NS * AB, NS * AB)


def transform_kernel(own_at, occupied, virtual, source, *refs):
    pairs, region = virtual.shape[:2]
    outs, (flipped, first) = list(refs[:-2]), refs[-2:]
    own = outs.pop(own_at) if own_at is not None else None
    group = 16
    few = 8

    def flip(g, _):
        at = pl.ds(pl.multiple_of(g * group, group), group)
        flipped[:, at, :] = jnp.swapaxes(source[at], 0, 1)
        return 0

    lax.fori_loop(0, region // group, flip, 0)

    def left(g, _):
        at = pl.ds(pl.multiple_of(g * group, group), group)
        for j in range(pairs):
            products = [
                jnp.dot(
                    occupied[j], flipped[g * group + k], preferred_element_type=jnp.float32
                ).astype(jnp.bfloat16)
                for k in range(group)
            ]
            first[j, :, at, :] = jnp.swapaxes(jnp.stack(products), 0, 1)
        return 0

    lax.fori_loop(0, region // group, left, 0)
    if own is not None:
        own[...] = jnp.zeros_like(own)

    def right(g, _):
        images = []
        for k in range(few):
            l = g * few + k
            for j in range(pairs):
                image = jnp.dot(
                    virtual[j], first[j, l], preferred_element_type=jnp.float32
                ).astype(jnp.bfloat16)
                if j == own_at:
                    images.append(image)
                else:
                    outs[j - (own_at is not None and j > own_at)][l] = image
        if own is not None:
            own[...] += lax.dot_general(
                jnp.concatenate(images, axis=0),
                source[pl.ds(g * few, few)].reshape(few * region, -1),
                (((0,), (0,)), ((), ())),
                preferred_element_type=jnp.float32,
            )
        return 0

    lax.fori_loop(0, region // few, right, 0)


def transform(occupied, virtual, source, own_at):
    region, _, width = source.shape
    pairs = virtual.shape[0]
    vmem = pl.BlockSpec(memory_space=pltpu.VMEM)
    image = jax.ShapeDtypeStruct((region, region, width), jnp.bfloat16)
    shapes = [image] * pairs
    if own_at is not None:
        shapes[own_at] = jax.ShapeDtypeStruct((width, width), jnp.float32)
    return pl.pallas_call(
        functools.partial(transform_kernel, own_at),
        out_shape=shapes,
        in_specs=[vmem] * 3,
        out_specs=[vmem] * pairs,
        scratch_shapes=[
            pltpu.VMEM((region, region, width), jnp.bfloat16),
            pltpu.VMEM((pairs, region, region, width), jnp.bfloat16),
        ],
        compiler_params=pltpu.CompilerParams(vmem_limit_bytes=40 * 2**20),
        cost_estimate=pl.CostEstimate(
            flops=12 * pairs * region**3 * width, bytes_accessed=8 * 2**20, transcendentals=0
        ),
        name="transform",
    )(occupied, virtual, source)


def contract_kernel(pieces, *refs):
    down, up = refs[:2]
    parts = refs[2 : 2 + pieces]
    chi_down, chi_up, held, sem = refs[2 + pieces :]
    region = held.shape[0]

    def bring(moves):
        copies = [
            pltpu.make_async_copy(source, held.at[pl.ds(start, source.shape[0])], sem.at[i])
            for i, (source, start) in enumerate(moves)
        ]
        for copy in copies:
            copy.start()
        for copy in copies:
            copy.wait()

    if pieces == 1:
        bring([(parts[0], 0)])
    else:
        t = lax.axis_index("tau")
        odd = lax.axis_index("blk") % 2
        step = parts[1].shape[0]

        @pl.when(odd == 0)
        def _():
            bring([(parts[0], 0)])

        @pl.when(odd == 1)
        def _():
            bring([(parts[1], t * (region - step)), (parts[2], step), (parts[3], (1 - t) * (region - step))])

    chi_down[...] = jnp.zeros_like(chi_down)
    chi_up[...] = jnp.zeros_like(chi_up)
    width = held.shape[2]
    rows = 8

    def body(g, _):
        def flat(ref):
            return ref[pl.ds(g * rows, rows)].reshape(rows * region, width)

        partner = flat(held)
        dims = (((0,), (0,)), ((), ()))
        chi_down[...] += lax.dot_general(partner, flat(down), dims, preferred_element_type=jnp.float32)
        chi_up[...] += lax.dot_general(flat(up), partner, dims, preferred_element_type=jnp.float32)
        return 0

    lax.fori_loop(0, region // rows, body, 0)


def contract(down, up, parts):
    region, _, width = down.shape
    vmem = pl.BlockSpec(memory_space=pltpu.VMEM)
    anywhere = pl.BlockSpec(memory_space=pl.ANY)
    chi = jax.ShapeDtypeStruct((width, width), jnp.float32)
    return pl.pallas_call(
        functools.partial(contract_kernel, len(parts)),
        out_shape=(chi, chi),
        in_specs=[vmem] * 2 + [anywhere] * len(parts),
        out_specs=(vmem, vmem),
        scratch_shapes=[pltpu.VMEM((region, region, width), jnp.bfloat16), pltpu.SemaphoreType.DMA((3,))],
        compiler_params=pltpu.CompilerParams(vmem_limit_bytes=32 * 2**20),
        cost_estimate=pl.CostEstimate(
            flops=4 * region**2 * width**2, bytes_accessed=12 * 2**20, transcendentals=0
        ),
        name="contract",
    )(down, up, *parts)


def exchange(chi, weights, step):
    taus = lax.axis_size("tau")
    blks = lax.axis_size("blk")
    t = lax.axis_index("tau")
    total = None
    for shift in range(taus):
        target = lax.rem(t + shift, taus)
        piece = lax.dynamic_index_in_dim(weights, target, 0, keepdims=False) * chi
        if shift or step:
            perm = [
                (i * blks + j, ((i + shift) % taus) * blks + (j + step) % blks)
                for i in range(taus)
                for j in range(blks)
            ]
            piece = lax.ppermute(piece, ("tau", "blk"), perm)
        total = piece if total is None else total + piece
    return total


def pull_ahead(value):
    taus = lax.axis_size("tau")
    blks = lax.axis_size("blk")
    rows = value.shape[0]
    if taus != 2 or blks % 2 or rows % 4:
        return [lax.ppermute(value, "blk", [(i, (i - 1) % blks) for i in range(blks)])]
    quarter = rows // 4
    evens = [(i, (i - 1) % blks) for i in range(0, blks, 2)]
    odds = [(i, i - 1) for i in range(1, blks, 2)]
    start = lax.axis_index("tau") * (rows - quarter)
    end = lax.ppermute(lax.dynamic_slice_in_dim(value, start, quarter, 0), "blk", evens)
    middle = lax.ppermute(value[quarter : rows - quarter], "blk", evens)
    return [lax.ppermute(value, "blk", odds), end, middle]


def swap_planes(end):
    blks = lax.axis_size("blk")
    pairs = [(i * blks + j, (1 - i) * blks + j) for i in range(2) for j in range(1, blks, 2)]
    return lax.ppermute(end, ("tau", "blk"), pairs)


def local(three_center, green_blocks, block_owner, block_slot, fold_weights):
    source = three_center[0]
    devices = lax.axis_size("blk")
    per_slot = NS * NS
    ids = block_owner * green_blocks.shape[1] + block_slot
    next_ids = lax.ppermute(ids[:per_slot], "blk", [(i, (i - 1) % devices) for i in range(devices)])
    table = lax.all_gather(green_blocks[0], "blk", axis=0, tiled=True)
    used = jnp.concatenate([next_ids, ids[per_slot:]])
    table, used, sent = lax.optimization_barrier((table, used, source))
    parts = pull_ahead(sent)
    fetched = table.at[used].get(mode="promise_in_bounds")
    occupied, virtual = green_pairs(fetched)
    weights = fold_weights[:, 0] * -2.0
    (down,) = transform(occupied[:1].swapaxes(1, 2), virtual[:1].swapaxes(1, 2), source, None)
    occupied, virtual = occupied[1:], virtual[1:]
    if len(parts) > 1:
        down, occupied, virtual, parts[1] = lax.optimization_barrier((down, occupied, virtual, parts[1]))
        parts.append(swap_planes(parts[1]))
    chi_own, up = transform(occupied, virtual, source, 0)
    out_own = exchange(chi_own, weights, 0)
    chi_down, chi_up = contract(down, up, parts)
    out_down = exchange(chi_down, weights, 1)
    out_up = exchange(chi_up, weights, 0)
    return jnp.concatenate([out_down, out_own, out_up], axis=1)[None]


def solution(mesh):
    return jax.shard_map(
        local,
        mesh=mesh,
        in_specs=(
            P("blk", None, None, None),
            P("tau", "blk", None),
            P("blk"),
            P("blk"),
            P(None, "tau"),
        ),
        out_specs=P("tau", "blk", None),
        check_vma=False,
    )
```

time: 144 us -> 103 us (0.72)
  Pallas kernels: 58.6 us -> 30.1 us
  waiting for transfers between devices: 24.8 us -> 9.32 us
  local copies, waits for them, and re-layouts: 13.3 us -> 17.5 us
  other arithmetic: 8.04 us -> 5.95 us
  blocking collectives: 19.3 us -> 20.8 us
    pallas_call x1 -> x2, Pallas kernels: 50.9 us -> 22.4 us  [transform(): pl.pallas_call(functools.partial(transform_kernel, own_at), out_shape=sha...]
    ppermute x5 -> x4, waiting for transfers between devices: 15.9 us -> 0.01 us  [the longest x1 0.01 us: swap_planes(): return lax.ppermute(end, ('tau', 'blk'), pairs)]
    slice x8 -> x9, local copies, waits for them, and re-layouts: 1.1 us -> 7.09 us  [the longest x1 3.19 us: pull_ahead(): middle = lax.ppermute(value[quarter:rows - quarter], 'blk', evens)]
    unnamed x6, local copies, waits for them, and re-layouts: 4.37 us -> 2.19 us
    ppermute x5 -> x4, starting transfers between devices: 10.3 us -> 9.5 us  [the longest x1 6.07 us: pull_ahead(): lax.ppermute(lax.dynamic_slice_in_dim(value, start, quarter, 0), 'blk', e...]
  transfers between devices with their start and end apart: 10 -> 9, of which waited for: 6 -> 4; matrix products, arithmetic and copies ran while one was open for 10% -> 19% of each run, Pallas kernels for 35% -> 22%
where the time goes in v4:
time: 103 us
  Pallas kernels  30.1 us (29%)
  blocking collectives  20.8 us (20%)
  starting transfers between devices  18.9 us (18%)
  local copies, waits for them, and re-layouts  17.5 us (17%)
  waiting for transfers between devices  9.32 us (9%)
  other arithmetic  5.95 us (6%)
    pallas_call x2, Pallas kernels, transform(): pl.pallas_call(functools.partial(transform_kernel, own_at), out_shape=sha...  22.4 us
    all_gather x1, blocking collectives, local(): table = lax.all_gather(green_blocks[0], 'blk', axis=0, tiled=True)  20.8 us
    ppermute x4, waiting for transfers between devices, exchange(): piece = lax.ppermute(piece, ('tau', 'blk'), perm)  9.31 us
    pallas_call x1, Pallas kernels, contract(): pl.pallas_call(functools.partial(contract_kernel, len(parts)), out_shape=...  7.72 us
    ppermute x1, starting transfers between devices, pull_ahead(): lax.ppermute(lax.dynamic_slice_in_dim(value, start, quarter, 0), 'blk', e...  6.07 us
    ppermute x1, starting transfers between devices, local(): lax.ppermute(ids[:per_slot], 'blk', [(i, (i - 1) % devices) for i in rang...  5.44 us
    ppermute x4, starting transfers between devices, exchange(): piece = lax.ppermute(piece, ('tau', 'blk'), perm)  3.92 us
    reshape x2, local copies, waits for them, and re-layouts, green_pairs(): blocks.reshape(count, NS, NS, 2, AB, AB).transpose(3, 0, 1, 4, 2, 5)  3.21 us
  transfers between devices with their start and end apart: 9, of which 4 were waited for; matrix products, arithmetic and copies ran while one was open for 19% of the time, Pallas kernels for 22%

profile of v4, /device:TPU:0, one launch (start us, length us, event | category | flops | bytes accessed | tf_op | source)
XLA Modules:
  0.0 102.7 jit_solution(13447888490894870099)
XLA Ops:
  0.0 0.7 multiply_add_fusion.2
  0.7 5.4 %collective-permute-start = (s32[16]{0:T(128)S(1)}, s32[16]{0:T(128)S(1)}, u32[]{:S(2)}, u32[]{:S(2)}) collective-permute-start(s32[16]{0:T(128)S(1)} %bitcast.22), channel_id=1, source_target_pairs={{0,15},{1,0},{2,1},{3,2},{4,3},{5,4},{6,5},{7,6},{8,7},{9,8},{10,9... | collective-permute-start | bytes 200 | tf_op jit(solution)/shard_map/ppermute | solution.py:212
  6.1 20.8 %all-gather = bf16[1,128,2048]{2,1,0:T(8,128)(2,1)} all-gather(bf16[1,8,2048]{2,1,0:T(8,128)(2,1)} %param.6), channel_id=2, replica_groups=mesh['tau'=2,'blk'=16] {'blk'}, dimensions={1}, use_global_device_ids=true | all-gather | bytes 557056 | tf_op jit(solution)/shard_map/all_gather | solution.py:213
  27.0 1.3 %collective-permute-start.2 = (bf16[128,128,128]{2,1,0:T(8,128)(2,1)}, bf16[128,128,128]{2,1,0:T(8,128)(2,1)}, u32[]{:S(2)}, u32[]{:S(2)}) collective-permute-start(bf16[128,128,128]{2,1,0:T(8,128)(2,1)} %bitcast.12), channel_id=1, source_target_pairs={{1,0},{3,2},{5,4},{7,6},{9,8},{11,10},{13,12},{15,14},{17,16},{19,... | collective-permute-start | bytes 12582920 | tf_op jit(solution)/shard_map/ppermute | solution.py:198
  28.3 0.7 broadcast_multiply_fusion.4
  29.6 3.2 %slice.49 = bf16[64,128,128]{2,1,0:T(8,128)(2,1)} slice(bf16[128,128,128]{2,1,0:T(8,128)(2,1)} %bitcast.13), slice={[32:96], [0:128], [0:128]} | slice | bytes 4194304 | tf_op jit(solution)/shard_map/slice | solution.py:197
  32.8 2.3 %constant_dynamic-slice_fusion.1 = bf16[32,128,128]{2,1,0:T(8,128)(2,1)} fusion(bf16[128,128,128]{2,1,0:T(8,128)(2,1)} %bitcast.14, s32[]{:T(128)S(6)} %select_n.19), kind=kLoop, calls=%fused_computation.12 | loop fusion | bytes 2097156 | tf_op jit(solution)/shard_map/dynamic_slice | solution.py:196
  35.1 6.1 %collective-permute-start.1 = (bf16[32,128,128]{2,1,0:T(8,128)(2,1)}, bf16[32,128,128]{2,1,0:T(8,128)(2,1)S(1)}, u32[]{:S(2)}, u32[]{:S(2)}) collective-permute-start(bf16[32,128,128]{2,1,0:T(8,128)(2,1)} %constant_dynamic-slice_fusion.1), channel_id=1, source_target_pairs={{0,15},{2,1},{4,3},{6,5},{8,7},{10,9},{12,11},{14,13},{16,31},{18,... | collective-permute-start | bytes 3145736 | tf_op jit(solution)/shard_map/ppermute | solution.py:196
  41.2 1.4 %collective-permute-start.3 = (bf16[64,128,128]{2,1,0:T(8,128)(2,1)}, bf16[64,128,128]{2,1,0:T(8,128)(2,1)S(1)}, u32[]{:S(2)}, u32[]{:S(2)}) collective-permute-start(bf16[64,128,128]{2,1,0:T(8,128)(2,1)} %slice.49), channel_id=1, source_target_pairs={{0,15},{2,1},{4,3},{6,5},{8,7},{10,9},{12,11},{14,13},{16,31},{18,... | collective-permute-start | bytes 6291464 | tf_op jit(solution)/shard_map/ppermute | solution.py:197
  42.6 2.0 %gather_fusion = bf16[48,2048]{1,0:T(8,128)(2,1)S(1)} fusion(bf16[128,2048]{1,0:T(8,128)(2,1)} %bitcast.19, s32[1024]{0:T(1024)S(1)} %pad_clamp_fusion), kind=kCustom, calls=%fused_computation | custom fusion | bytes 393408 | tf_op jit(solution)/shard_map/gather | solution.py:217
  44.6 1.5 %reshape.18 = bf16[3,4,4,2,32,32]{5,4,3,2,1,0:T(8,128)(2,1)} reshape(bf16[48,2048]{1,0:T(8,128)(2,1)S(1)} %gather_fusion) | data formatting | bytes 393216 | tf_op jit(solution)/shard_map/reshape | solution.py:16
  46.1 1.7 %copy.12 = bf16[3,4,4,2,32,32]{5,2,4,1,0,3:T(4,128)(2,1)S(1)} copy(bf16[3,4,4,2,32,32]{5,4,3,2,1,0:T(8,128)(2,1)} %reshape.18) | data formatting | bytes 393216 | tf_op jit(solution)/shard_map/reshape | solution.py:16
  47.9 1.0 %fusion = (bf16[1,2,4,32,4,32]{5,4,3,2,1,0:T(4,128)(2,1)S(1)}, bf16[1,2,4,32,4,32]{5,4,3,2,1,0:T(4,128)(2,1)}) fusion(bf16[2,3,4,32,4,32]{5,4,3,2,1,0:T(4,128)(2,1)S(1)} %bitcast.20), kind=kLoop, calls=%fused_computation.17 | loop fusion | bytes 262144 | tf_op jit(solution)/shard_map/slice | solution.py:221
  49.1 1.1 %fusion.1 = (bf16[1,1,4,32,4,32]{5,4,3,2,1,0:T(4,128)(2,1)S(1)}, bf16[1,1,4,32,4,32]{5,4,3,2,1,0:T(4,128)(2,1)S(1)}) fusion(bf16[2,3,4,32,4,32]{5,4,3,2,1,0:T(4,128)(2,1)} %bitcast.21), kind=kLoop, calls=%fused_computation.18 | loop fusion | bytes 131072 | tf_op jit(solution)/shard_map/slice | solution.py:220
  50.6 1.2 %slice.46.occupied = bf16[2,128,128]{2,1,0:T(8,128)(2,1)S(1)} reshape(bf16[1,2,4,32,4,32]{5,4,3,2,1,0:T(4,128)(2,1)} %get-tuple-element.28) | data formatting | bytes 131072 | tf_op jit(solution)/shard_map/slice | solution.py:221
  51.8 2.2 %copy-done = bf16[1,128,128,128]{3,2,1,0:T(8,128)(2,1)S(1)} copy-done((bf16[1,128,128,128]{3,2,1,0:T(8,128)(2,1)S(1)}, bf16[1,128,128,128]{3,2,1,0:T(8,128)(2,1)}, u32[]{:S(2)}) %copy-start) | copy-done | bytes 4194328
  54.0 8.2 %transform.2.refs_0_ = bf16[128,128,128]{2,1,0:T(8,128)(2,1)S(1)} custom-call(bf16[1,128,128]{2,1,0:T(8,128)(2,1)S(1)} %bitcast.18, bf16[1,128,128]{2,1,0:T(8,128)(2,1)S(1)} %bitcast.17, bf16[128,128,128]{2,1,0:T(8,128)(2,1)S(1)} %bitcast.15), custom_call_target="tpu_custom_call" | custom-call | flops 3221225472 | bytes 8388608 | tf_op jit(solution)/shard_map/transform/pallas_call | solution.py:82
  62.2 0.7 collective-permute-start.4
  63.0 14.2 %transform.3 = (f32[128,128]{1,0:T(8,128)S(1)}, bf16[128,128,128]{2,1,0:T(8,128)(2,1)S(1)}) custom-call(bf16[2,128,128]{2,1,0:T(8,128)(2,1)S(1)} %slice.46.occupied, bf16[2,128,128]{2,1,0:T(8,128)(2,1)S(1)} %slice.48.virtual, bf16[128,128,128]{2,1,0:T(8,128)(2,1)S(1)} %bitcast.16), custom_call_target="tpu_custom_call" | custom-call | flops 6442450944 | bytes 8388608 | tf_op jit(solution)/shard_map/transform/pallas_call | solution.py:82
  77.2 0.6 broadcast_multiply_fusion.1
  77.8 1.6 %collective-permute-start.7 = (f32[128,128]{1,0:T(8,128)S(1)}, f32[128,128]{1,0:T(8,128)S(1)}, u32[]{:S(2)}, u32[]{:S(2)}) collective-permute-start(f32[128,128]{1,0:T(8,128)S(1)} %broadcast_multiply_fusion.1), channel_id=1, source_target_pairs={{0,16},{1,17},{2,18},{3,19},{4,20},{5,21},{6,22},{7,23},{8,24},{9,... | collective-permute-start | bytes 196616 | tf_op jit(solution)/shard_map/ppermute | solution.py:181
  79.3 3.1 %collective-permute-done.7 = f32[128,128]{1,0:T(8,128)S(1)} collective-permute-done((f32[128,128]{1,0:T(8,128)S(1)}, f32[128,128]{1,0:T(8,128)S(1)}, u32[]{:S(2)}, u32[]{:S(2)}) %collective-permute-start.7) | collective-permute-done | bytes 65568 | tf_op jit(solution)/shard_map/ppermute | solution.py:181
  82.4 0.7 multiply_add_fusion.1
  83.1 7.7 %contract.1 = (f32[128,128]{1,0:T(8,128)S(1)}, f32[128,128]{1,0:T(8,128)S(1)}) custom-call(bf16[128,128,128]{2,1,0:T(8,128)(2,1)S(1)} %transform.2.refs_0_, bf16[128,128,128]{2,1,0:T(8,128)(2,1)S(1)} %get-tuple-element.22.refs_1_, bf16[128,128,128]{2,1,0:T(8,128)(2,1)} %collective-permute-done.2.refs_2_, ...), custom_call_target="tpu_custom_call" | custom-call | flops 1073741824 | bytes 12582912 | tf_op jit(solution)/shard_map/contract/pallas_call | solution.py:153
  90.8 0.6 broadcast_multiply_fusion
  91.4 1.3 %collective-permute-start.8 = (f32[128,128]{1,0:T(8,128)S(1)}, f32[128,128]{1,0:T(8,128)S(1)}, u32[]{:S(2)}, u32[]{:S(2)}) collective-permute-start(f32[128,128]{1,0:T(8,128)S(1)} %broadcast_multiply_fusion), channel_id=1, source_target_pairs={{0,16},{1,17},{2,18},{3,19},{4,20},{5,21},{6,22},{7,23},{8,24},{9,... | collective-permute-start | bytes 196616 | tf_op jit(solution)/shard_map/ppermute | solution.py:181
  92.7 1.3 %broadcast_multiply_fusion.2 = (f32[128,128]{1,0:T(8,128)S(1)}, f32[128,128]{1,0:T(8,128)S(1)}) fusion(f32[128,128]{1,0:T(8,128)S(1)} %get-tuple-element.24, f32[]{:T(128)} %bitcast.6, f32[]{:T(128)} %bitcast), kind=kLoop, calls=%fused_computation.7 | loop fusion | flops 32768 | bytes 196616 | tf_op jit(solution)/shard_map/mul | solution.py:174
  94.0 1.1 %collective-permute-start.5 = (f32[128,128]{1,0:T(8,128)S(1)}, f32[128,128]{1,0:T(8,128)S(1)}, u32[]{:S(2)}, u32[]{:S(2)}) collective-permute-start(f32[128,128]{1,0:T(8,128)S(1)} %get-tuple-element.32), channel_id=1, source_target_pairs={{0,1},{1,2},{2,3},{3,4},{4,5},{5,6},{6,7},{7,8},{8,9},{9,10},{10,1... | collective-permute-start | bytes 196616 | tf_op jit(solution)/shard_map/ppermute | solution.py:181
  95.1 0.7 collective-permute-done.8
  95.8 0.7 multiply_add_fusion
  96.4 5.5 %collective-permute-done.6 = f32[128,128]{1,0:T(8,128)S(1)} collective-permute-done((f32[128,128]{1,0:T(8,128)S(1)}, f32[128,128]{1,0:T(8,128)S(1)}, u32[]{:S(2)}, u32[]{:S(2)}) %collective-permute-start.6) | collective-permute-done | bytes 65568 | tf_op jit(solution)/shard_map/ppermute | solution.py:181
  102.0 0.7 maximum_bitcast_fusion
  (23 shorter events, 1.6 us)
Async XLA Ops:
  0.7 26.3 %collective-permute-start = (s32[16]{0:T(128)S(1)}, s32[16]{0:T(128)S(1)}, u32[]{:S(2)}, u32[]{:S(2)}) collective-permute-start(s32[16]{0:T(128)S(1)} %bitcast.22), channel_id=1, source_target_pairs={{0,15},{1,0},{2,1},{3,2},{4,3},{5,4},{6,5},{7,6},{8,7},{9,8},{10,9... | collective-permute-start | bytes 200 | tf_op jit(solution)/shard_map/ppermute | solution.py:212
  27.0 56.1 %collective-permute-start.2 = (bf16[128,128,128]{2,1,0:T(8,128)(2,1)}, bf16[128,128,128]{2,1,0:T(8,128)(2,1)}, u32[]{:S(2)}, u32[]{:S(2)}) collective-permute-start(bf16[128,128,128]{2,1,0:T(8,128)(2,1)} %bitcast.12), channel_id=1, source_target_pairs={{1,0},{3,2},{5,4},{7,6},{9,8},{11,10},{13,12},{15,14},{17,16},{19,... | collective-permute-start | bytes 12582920 | tf_op jit(solution)/shard_map/ppermute | solution.py:198
  35.1 27.1 %collective-permute-start.1 = (bf16[32,128,128]{2,1,0:T(8,128)(2,1)}, bf16[32,128,128]{2,1,0:T(8,128)(2,1)S(1)}, u32[]{:S(2)}, u32[]{:S(2)}) collective-permute-start(bf16[32,128,128]{2,1,0:T(8,128)(2,1)} %constant_dynamic-slice_fusion.1), channel_id=1, source_target_pairs={{0,15},{2,1},{4,3},{6,5},{8,7},{10,9},{12,11},{14,13},{16,31},{18,... | collective-permute-start | bytes 3145736 | tf_op jit(solution)/shard_map/ppermute | solution.py:196
  41.2 41.9 %collective-permute-start.3 = (bf16[64,128,128]{2,1,0:T(8,128)(2,1)}, bf16[64,128,128]{2,1,0:T(8,128)(2,1)S(1)}, u32[]{:S(2)}, u32[]{:S(2)}) collective-permute-start(bf16[64,128,128]{2,1,0:T(8,128)(2,1)} %slice.49), channel_id=1, source_target_pairs={{0,15},{2,1},{4,3},{6,5},{8,7},{10,9},{12,11},{14,13},{16,31},{18,... | collective-permute-start | bytes 6291464 | tf_op jit(solution)/shard_map/ppermute | solution.py:197
  47.8 1.0 %copy-start.2 = (bf16[3,4,4,2,32,32]{5,2,4,1,0,3:T(4,128)(2,1)}, bf16[3,4,4,2,32,32]{5,2,4,1,0,3:T(4,128)(2,1)S(1)}, u32[]{:S(2)}) copy-start(bf16[3,4,4,2,32,32]{5,2,4,1,0,3:T(4,128)(2,1)S(1)} %copy.12) | copy-start | bytes 589828
  51.8 2.2 %copy-start = (bf16[1,128,128,128]{3,2,1,0:T(8,128)(2,1)S(1)}, bf16[1,128,128,128]{3,2,1,0:T(8,128)(2,1)}, u32[]{:S(2)}) copy-start(bf16[1,128,128,128]{3,2,1,0:T(8,128)(2,1)} %param.5) | copy-start | bytes 12582916
  54.0 9.0 %copy-start.1 = (bf16[1,128,128,128]{3,2,1,0:T(8,128)(2,1)S(1)}, bf16[1,128,128,128]{3,2,1,0:T(8,128)(2,1)}, u32[]{:S(2)}) copy-start(bf16[1,128,128,128]{3,2,1,0:T(8,128)(2,1)} %param.5) | copy-start | bytes 12582916
  62.2 20.8 %collective-permute-start.4 = (bf16[32,128,128]{2,1,0:T(8,128)(2,1)S(1)}, bf16[32,128,128]{2,1,0:T(8,128)(2,1)S(1)}, u32[]{:S(2)}, u32[]{:S(2)}) collective-permute-start(bf16[32,128,128]{2,1,0:T(8,128)(2,1)S(1)} %collective-permute-done.1.refs_3_), channel_id=1, source_target_pairs={{1,17},{3,19},{5,21},{7,23},{9,25},{11,27},{13,29},{15,31},{17,1},... | collective-permute-start | bytes 3145736 | tf_op jit(solution)/shard_map/ppermute | solution.py:204
  77.8 4.6 %collective-permute-start.7 = (f32[128,128]{1,0:T(8,128)S(1)}, f32[128,128]{1,0:T(8,128)S(1)}, u32[]{:S(2)}, u32[]{:S(2)}) collective-permute-start(f32[128,128]{1,0:T(8,128)S(1)} %broadcast_multiply_fusion.1), channel_id=1, source_target_pairs={{0,16},{1,17},{2,18},{3,19},{4,20},{5,21},{6,22},{7,23},{8,24},{9,... | collective-permute-start | bytes 196616 | tf_op jit(solution)/shard_map/ppermute | solution.py:181
  91.4 4.3 %collective-permute-start.8 = (f32[128,128]{1,0:T(8,128)S(1)}, f32[128,128]{1,0:T(8,128)S(1)}, u32[]{:S(2)}, u32[]{:S(2)}) collective-permute-start(f32[128,128]{1,0:T(8,128)S(1)} %broadcast_multiply_fusion), channel_id=1, source_target_pairs={{0,16},{1,17},{2,18},{3,19},{4,20},{5,21},{6,22},{7,23},{8,24},{9,... | collective-permute-start | bytes 196616 | tf_op jit(solution)/shard_map/ppermute | solution.py:181
  94.0 8.0 %collective-permute-start.6 = (f32[128,128]{1,0:T(8,128)S(1)}, f32[128,128]{1,0:T(8,128)S(1)}, u32[]{:S(2)}, u32[]{:S(2)}) collective-permute-start(f32[128,128]{1,0:T(8,128)S(1)} %get-tuple-element.31), channel_id=1, source_target_pairs={{0,17},{1,18},{2,19},{3,20},{4,21},{5,22},{6,23},{7,24},{8,25},{9,... | collective-permute-start | bytes 196616 | tf_op jit(solution)/shard_map/ppermute | solution.py:181
  94.0 8.0 %collective-permute-start.5 = (f32[128,128]{1,0:T(8,128)S(1)}, f32[128,128]{1,0:T(8,128)S(1)}, u32[]{:S(2)}, u32[]{:S(2)}) collective-permute-start(f32[128,128]{1,0:T(8,128)S(1)} %get-tuple-element.32), channel_id=1, source_target_pairs={{0,1},{1,2},{2,3},{3,4},{4,5},{5,6},{6,7},{7,8},{8,9},{9,10},{10,1... | collective-permute-start | bytes 196616 | tf_op jit(solution)/shard_map/ppermute | solution.py:181

commit v5 on v4

--- a/solution.py
+++ b/solution.py
@@ -9,6 +9,7 @@
 
 AB = 32
 NS = 4
+LANES = 128
 
 
 def green_pairs(blocks):
@@ -168,7 +169,7 @@
     taus = lax.axis_size("tau")
     blks = lax.axis_size("blk")
     t = lax.axis_index("tau")
-    total = None
+    pieces = []
     for shift in range(taus):
         target = lax.rem(t + shift, taus)
         piece = lax.dynamic_index_in_dim(weights, target, 0, keepdims=False) * chi
@@ -179,8 +180,8 @@
                 for j in range(blks)
             ]
             piece = lax.ppermute(piece, ("tau", "blk"), perm)
-        total = piece if total is None else total + piece
-    return total
+        pieces.append(piece)
+    return pieces
 
 
 def pull_ahead(value):
@@ -208,13 +209,20 @@
     source = three_center[0]
     devices = lax.axis_size("blk")
     per_slot = NS * NS
-    ids = block_owner * green_blocks.shape[1] + block_slot
-    next_ids = lax.ppermute(ids[:per_slot], "blk", [(i, (i - 1) % devices) for i in range(devices)])
-    table = lax.all_gather(green_blocks[0], "blk", axis=0, tiled=True)
+    slots, length = green_blocks.shape[1:]
+    ids = block_owner * slots + block_slot
+    asked = jnp.concatenate([block_owner[:per_slot], block_slot[:per_slot]]).astype(jnp.bfloat16)
+    riders = jnp.broadcast_to(jnp.pad(asked, (0, LANES - 2 * per_slot)), (slots, LANES))
+    table = lax.all_gather(
+        jnp.concatenate([green_blocks[0], riders], axis=1), "blk", axis=0, tiled=True
+    )
+    table, sent = lax.optimization_barrier((table, source))
+    ahead = lax.rem(lax.axis_index("blk") + 1, devices)
+    asked = lax.dynamic_slice(table, (ahead * slots, length), (1, 2 * per_slot))[0].astype(jnp.int32)
+    next_ids = asked[:per_slot] * slots + asked[per_slot:]
     used = jnp.concatenate([next_ids, ids[per_slot:]])
-    table, used, sent = lax.optimization_barrier((table, used, source))
     parts = pull_ahead(sent)
-    fetched = table.at[used].get(mode="promise_in_bounds")
+    fetched = table.at[used].get(mode="promise_in_bounds")[:, :length]
     occupied, virtual = green_pairs(fetched)
     weights = fold_weights[:, 0] * -2.0
     (down,) = transform(occupied[:1].swapaxes(1, 2), virtual[:1].swapaxes(1, 2), source, None)
@@ -223,11 +231,12 @@
         down, occupied, virtual, parts[1] = lax.optimization_barrier((down, occupied, virtual, parts[1]))
         parts.append(swap_planes(parts[1]))
     chi_own, up = transform(occupied, virtual, source, 0)
-    out_own = exchange(chi_own, weights, 0)
+    own = exchange(chi_own, weights, 0)
     chi_down, chi_up = contract(down, up, parts)
-    out_down = exchange(chi_down, weights, 1)
-    out_up = exchange(chi_up, weights, 0)
-    return jnp.concatenate([out_down, out_own, out_up], axis=1)[None]
+    chi_down, chi_up, own = lax.optimization_barrier((chi_down, chi_up, own))
+    down = exchange(chi_down, weights, 1)
+    up = exchange(chi_up, weights, 0)
+    return jnp.concatenate([sum(down), sum(own), sum(up)], axis=1)[None]
 
 
 def solution(mesh):

time: 103 us -> 100 us (0.971)
  waiting for transfers between devices: 9.32 us -> 3.53 us
  starting transfers between devices: 18.9 us -> 13.3 us
  blocking collectives: 20.8 us -> 26.1 us
  local copies, waits for them, and re-layouts: 17.5 us -> 19.2 us
  other arithmetic: 5.95 us -> 7 us
    ppermute x4, waiting for transfers between devices: 9.31 us -> 3.51 us  [exchange(): piece = lax.ppermute(piece, ('tau', 'blk'), perm)]
    ppermute x1 -> x0, starting transfers between devices: 5.44 us -> none  [local(): lax.ppermute(ids[:per_slot], 'blk', [(i, (i - 1) % devices) for i in rang...]
    all_gather x1, blocking collectives: 20.8 us -> 26.1 us  [local(): lax.all_gather(jnp.concatenate([green_blocks[0], riders], axis=1), 'blk',...]
    ppermute x1, starting transfers between devices: 6.07 us -> 3.84 us  [pull_ahead(): lax.ppermute(lax.dynamic_slice_in_dim(value, start, quarter, 0), 'blk', e...]
    ppermute x4, starting transfers between devices: 3.92 us -> 6.06 us  [exchange(): piece = lax.ppermute(piece, ('tau', 'blk'), perm)]
    slice x3, local copies, waits for them, and re-layouts: 1.3 us -> 2.87 us  [local(): virtual[:1].swapaxes(1, 2)]
    unnamed x6 -> x8, local copies, waits for them, and re-layouts: 2.19 us -> 2.19 us
  transfers between devices with their start and end apart: 9 -> 8, of which waited for: 4 -> 2; matrix products, arithmetic and copies ran while one was open for 19% -> 21% of each run, Pallas kernels for 22% -> 30%
where the time goes in v5:
time: 100 us; the launch traced here: 99.4 us
  Pallas kernels  30.1 us (30%)
  blocking collectives  26.1 us (26%)
  local copies, waits for them, and re-layouts  19.2 us (19%)
  starting transfers between devices  13.3 us (13%)
  other arithmetic  7 us (7%)
  waiting for transfers between devices  3.53 us (4%)
    all_gather x1, blocking collectives, local(): lax.all_gather(jnp.concatenate([green_blocks[0], riders], axis=1), 'blk',...  26.1 us
    pallas_call x2, Pallas kernels, transform(): pl.pallas_call(functools.partial(transform_kernel, own_at), out_shape=sha...  22.4 us
    pallas_call x1, Pallas kernels, contract(): pl.pallas_call(functools.partial(contract_kernel, len(parts)), out_shape=...  7.72 us
    ppermute x4, starting transfers between devices, exchange(): piece = lax.ppermute(piece, ('tau', 'blk'), perm)  6.06 us
    ppermute x1, starting transfers between devices, pull_ahead(): lax.ppermute(lax.dynamic_slice_in_dim(value, start, quarter, 0), 'blk', e...  3.84 us
    ppermute x4, waiting for transfers between devices, exchange(): piece = lax.ppermute(piece, ('tau', 'blk'), perm)  3.51 us
    reshape x2, local copies, waits for them, and re-layouts, green_pairs(): blocks.reshape(count, NS, NS, 2, AB, AB).transpose(3, 0, 1, 4, 2, 5)  3.23 us
    mul x3, other arithmetic, exchange(): piece = lax.dynamic_index_in_dim(weights, target, 0, keepdims=False) * chi  3.22 us
  transfers between devices with their start and end apart: 8, of which 2 were waited for; matrix products, arithmetic and copies ran while one was open for 21% of the time, Pallas kernels for 30%

profile of v5, /device:TPU:0, one launch (start us, length us, event | category | flops | bytes accessed | tf_op | source)
XLA Modules:
  0.0 99.4 jit_solution(2697771596197569253)
XLA Ops:
  0.0 0.7 multiply_add_fusion.1
  0.8 0.8 pad_maximum_fusion
  1.6 26.1 %all_gather.3 = bf16[128,2176]{1,0:T(8,128)(2,1)} all-gather(bf16[8,2176]{1,0:T(8,128)(2,1)S(1)} %pad_maximum_fusion), channel_id=1, replica_groups=mesh['tau'=2,'blk'=16] {'blk'}, dimensions={0}, use_global_device_ids=true | all-gather | bytes 591872 | tf_op jit(solution)/shard_map/all_gather | solution.py:216
  27.7 1.3 %collective-permute-start.1 = (bf16[128,128,128]{2,1,0:T(8,128)(2,1)}, bf16[128,128,128]{2,1,0:T(8,128)(2,1)}, u32[]{:S(2)}, u32[]{:S(2)}) collective-permute-start(bf16[128,128,128]{2,1,0:T(8,128)(2,1)} %bitcast.19), channel_id=1, source_target_pairs={{1,0},{3,2},{5,4},{7,6},{9,8},{11,10},{13,12},{15,14},{17,16},{19,... | collective-permute-start | bytes 12582920 | tf_op jit(solution)/shard_map/ppermute | solution.py:199
  29.0 2.3 %constant_dynamic-slice_fusion.1 = bf16[32,128,128]{2,1,0:T(8,128)(2,1)} fusion(bf16[128,128,128]{2,1,0:T(8,128)(2,1)} %bitcast.20, s32[]{:T(128)S(6)} %select_n.30), kind=kLoop, calls=%fused_computation.15 | loop fusion | bytes 2097156 | tf_op jit(solution)/shard_map/dynamic_slice | solution.py:197
  31.3 3.8 %collective-permute-start = (bf16[32,128,128]{2,1,0:T(8,128)(2,1)}, bf16[32,128,128]{2,1,0:T(8,128)(2,1)S(1)}, u32[]{:S(2)}, u32[]{:S(2)}) collective-permute-start(bf16[32,128,128]{2,1,0:T(8,128)(2,1)} %constant_dynamic-slice_fusion.1), channel_id=1, source_target_pairs={{0,15},{2,1},{4,3},{6,5},{8,7},{10,9},{12,11},{14,13},{16,31},{18,... | collective-permute-start | bytes 3145736 | tf_op jit(solution)/shard_map/ppermute | solution.py:197
  35.1 3.2 %slice.69 = bf16[64,128,128]{2,1,0:T(8,128)(2,1)} slice(bf16[128,128,128]{2,1,0:T(8,128)(2,1)} %bitcast.21), slice={[32:96], [0:128], [0:128]} | slice | bytes 4194304 | tf_op jit(solution)/shard_map/slice | solution.py:198
  38.4 1.4 %collective-permute-start.2 = (bf16[64,128,128]{2,1,0:T(8,128)(2,1)}, bf16[64,128,128]{2,1,0:T(8,128)(2,1)S(1)}, u32[]{:S(2)}, u32[]{:S(2)}) collective-permute-start(bf16[64,128,128]{2,1,0:T(8,128)(2,1)} %slice.69), channel_id=1, source_target_pairs={{0,15},{2,1},{4,3},{6,5},{8,7},{10,9},{12,11},{14,13},{16,31},{18,... | collective-permute-start | bytes 6291464 | tf_op jit(solution)/shard_map/ppermute | solution.py:198
  39.8 0.7 dynamic-slice_convert_fusion
  40.7 2.0 %gather_fusion = bf16[48,2176]{1,0:T(8,128)(2,1)S(1)} fusion(bf16[128,2176]{1,0:T(8,128)(2,1)} %all_gather.3, s32[1024]{0:T(1024)S(1)} %pad_clamp_fusion), kind=kCustom, calls=%fused_computation | custom fusion | bytes 417984 | tf_op jit(solution)/shard_map/gather | solution.py:225
  42.8 1.5 %reshape.108 = bf16[3,4,4,2,32,32]{5,4,3,2,1,0:T(8,128)(2,1)} reshape(bf16[48,2048]{1,0:T(8,128)(2,1)S(1)} %slice.72) | data formatting | bytes 393216 | tf_op jit(solution)/shard_map/reshape | solution.py:17
  44.2 1.7 %copy.12 = bf16[3,4,4,2,32,32]{5,2,4,1,0,3:T(4,128)(2,1)S(1)} copy(bf16[3,4,4,2,32,32]{5,4,3,2,1,0:T(8,128)(2,1)} %reshape.108) | data formatting | bytes 393216 | tf_op jit(solution)/shard_map/reshape | solution.py:17
  46.0 1.0 %fusion.2 = (bf16[1,2,4,32,4,32]{5,4,3,2,1,0:T(4,128)(2,1)S(1)}, bf16[1,2,4,32,4,32]{5,4,3,2,1,0:T(4,128)(2,1)}) fusion(bf16[2,3,4,32,4,32]{5,4,3,2,1,0:T(4,128)(2,1)S(1)} %bitcast.26), kind=kLoop, calls=%fused_computation.24 | loop fusion | bytes 262144 | tf_op jit(solution)/shard_map/slice | solution.py:229
  47.2 1.7 %fusion.3 = (bf16[1,1,4,32,4,32]{5,4,3,2,1,0:T(4,128)(2,1)}, bf16[1,1,4,32,4,32]{5,4,3,2,1,0:T(4,128)(2,1)S(1)}) fusion(bf16[2,3,4,32,4,32]{5,4,3,2,1,0:T(4,128)(2,1)} %bitcast.27), kind=kLoop, calls=%fused_computation.25 | loop fusion | bytes 131072 | tf_op jit(solution)/shard_map/slice | solution.py:228
  48.9 1.0 %reshape.118 = bf16[1,128,128]{2,1,0:T(8,128)(2,1)S(1)} reshape(bf16[1,1,4,32,4,32]{5,4,3,2,1,0:T(4,128)(2,1)} %get-tuple-element.35) | data formatting | bytes 65536 | tf_op jit(solution)/shard_map/slice | solution.py:228
  50.4 1.2 %slice.66.occupied = bf16[2,128,128]{2,1,0:T(8,128)(2,1)S(1)} reshape(bf16[1,2,4,32,4,32]{5,4,3,2,1,0:T(4,128)(2,1)} %get-tuple-element.34) | data formatting | bytes 131072 | tf_op jit(solution)/shard_map/slice | solution.py:229
  51.6 2.2 %copy-done = bf16[1,128,128,128]{3,2,1,0:T(8,128)(2,1)S(1)} copy-done((bf16[1,128,128,128]{3,2,1,0:T(8,128)(2,1)S(1)}, bf16[1,128,128,128]{3,2,1,0:T(8,128)(2,1)}, u32[]{:S(2)}) %copy-start) | copy-done | bytes 4194328
  53.7 8.2 %transform.2.refs_0_ = bf16[128,128,128]{2,1,0:T(8,128)(2,1)S(1)} custom-call(bf16[1,128,128]{2,1,0:T(8,128)(2,1)S(1)} %bitcast.25, bf16[1,128,128]{2,1,0:T(8,128)(2,1)S(1)} %bitcast.24, bf16[128,128,128]{2,1,0:T(8,128)(2,1)S(1)} %bitcast.22), custom_call_target="tpu_custom_call" | custom-call | flops 3221225472 | bytes 8388608 | tf_op jit(solution)/shard_map/transform/pallas_call | solution.py:83
  62.0 0.7 collective-permute-start.3
  62.7 0.6 constant_dynamic-slice_fusion
  63.3 14.2 %transform.3 = (f32[128,128]{1,0:T(8,128)S(1)}, bf16[128,128,128]{2,1,0:T(8,128)(2,1)S(1)}) custom-call(bf16[2,128,128]{2,1,0:T(8,128)(2,1)S(1)} %slice.66.occupied, bf16[2,128,128]{2,1,0:T(8,128)(2,1)S(1)} %slice.68.virtual, bf16[128,128,128]{2,1,0:T(8,128)(2,1)S(1)} %bitcast.23), custom_call_target="tpu_custom_call" | custom-call | flops 6442450944 | bytes 8388608 | tf_op jit(solution)/shard_map/transform/pallas_call | solution.py:83
  77.5 1.3 %broadcast_multiply_fusion.2 = (f32[128,128]{1,0:T(8,128)S(1)}, f32[128,128]{1,0:T(8,128)S(1)}) fusion(f32[128,128]{1,0:T(8,128)S(1)} %get-tuple-element.28, f32[]{:T(128)} %bitcast.9, f32[]{:T(128)} %bitcast), kind=kLoop, calls=%fused_computation.7 | loop fusion | flops 32768 | bytes 196616 | tf_op jit(solution)/shard_map/mul | solution.py:175
  78.8 1.6 %collective-permute-start.4 = (f32[128,128]{1,0:T(8,128)S(1)}, f32[128,128]{1,0:T(8,128)S(1)}, u32[]{:S(2)}, u32[]{:S(2)}) collective-permute-start(f32[128,128]{1,0:T(8,128)S(1)} %get-tuple-element.39), channel_id=1, source_target_pairs={{0,16},{1,17},{2,18},{3,19},{4,20},{5,21},{6,22},{7,23},{8,24},{9,... | collective-permute-start | bytes 196616 | tf_op jit(solution)/shard_map/ppermute | solution.py:182
  80.4 7.7 %contract.1 = (f32[128,128]{1,0:T(8,128)S(1)}, f32[128,128]{1,0:T(8,128)S(1)}) custom-call(bf16[128,128,128]{2,1,0:T(8,128)(2,1)S(1)} %transform.2.refs_0_, bf16[128,128,128]{2,1,0:T(8,128)(2,1)S(1)} %get-tuple-element.24.refs_1_, bf16[128,128,128]{2,1,0:T(8,128)(2,1)} %collective-permute-done.1.refs_2_, ...), custom_call_target="tpu_custom_call" | custom-call | flops 1073741824 | bytes 12582912 | tf_op jit(solution)/shard_map/contract/pallas_call | solution.py:154
  88.1 0.7 broadcast_multiply_fusion
  88.8 0.6 collective-permute-start.7
  89.4 1.3 %broadcast_multiply_fusion.1 = (f32[128,128]{1,0:T(8,128)S(1)}, f32[128,128]{1,0:T(8,128)S(1)}) fusion(f32[128,128]{1,0:T(8,128)S(1)} %get-tuple-element.29, f32[]{:T(128)} %bitcast.9, f32[]{:T(128)} %bitcast), kind=kLoop, calls=%fused_computation.6 | loop fusion | flops 32768 | bytes 196616 | tf_op jit(solution)/shard_map/mul | solution.py:175
  91.1 3.4 %collective-permute-start.5 = (f32[128,128]{1,0:T(8,128)S(1)}, f32[128,128]{1,0:T(8,128)S(1)}, u32[]{:S(2)}, u32[]{:S(2)}) collective-permute-start(f32[128,128]{1,0:T(8,128)S(1)} %get-tuple-element.38), channel_id=1, source_target_pairs={{0,1},{1,2},{2,3},{3,4},{4,5},{5,6},{6,7},{7,8},{8,9},{9,10},{10,1... | collective-permute-start | bytes 196616 | tf_op jit(solution)/shard_map/ppermute | solution.py:182
  94.6 0.6 multiply_add_fusion
  95.2 2.8 %collective-permute-done.6 = f32[128,128]{1,0:T(8,128)S(1)} collective-permute-done((f32[128,128]{1,0:T(8,128)S(1)}, f32[128,128]{1,0:T(8,128)S(1)}, u32[]{:S(2)}, u32[]{:S(2)}) %collective-permute-start.6) | collective-permute-done | bytes 65568 | tf_op jit(solution)/shard_map/ppermute | solution.py:182
  98.0 0.7 collective-permute-done.5
  98.7 0.7 maximum_bitcast_fusion
  (28 shorter events, 1.4 us)
Async XLA Ops:
  27.7 52.7 %collective-permute-start.1 = (bf16[128,128,128]{2,1,0:T(8,128)(2,1)}, bf16[128,128,128]{2,1,0:T(8,128)(2,1)}, u32[]{:S(2)}, u32[]{:S(2)}) collective-permute-start(bf16[128,128,128]{2,1,0:T(8,128)(2,1)} %bitcast.19), channel_id=1, source_target_pairs={{1,0},{3,2},{5,4},{7,6},{9,8},{11,10},{13,12},{15,14},{17,16},{19,... | collective-permute-start | bytes 12582920 | tf_op jit(solution)/shard_map/ppermute | solution.py:199
  31.3 30.7 %collective-permute-start = (bf16[32,128,128]{2,1,0:T(8,128)(2,1)}, bf16[32,128,128]{2,1,0:T(8,128)(2,1)S(1)}, u32[]{:S(2)}, u32[]{:S(2)}) collective-permute-start(bf16[32,128,128]{2,1,0:T(8,128)(2,1)} %constant_dynamic-slice_fusion.1), channel_id=1, source_target_pairs={{0,15},{2,1},{4,3},{6,5},{8,7},{10,9},{12,11},{14,13},{16,31},{18,... | collective-permute-start | bytes 3145736 | tf_op jit(solution)/shard_map/ppermute | solution.py:197
  38.4 42.0 %collective-permute-start.2 = (bf16[64,128,128]{2,1,0:T(8,128)(2,1)}, bf16[64,128,128]{2,1,0:T(8,128)(2,1)S(1)}, u32[]{:S(2)}, u32[]{:S(2)}) collective-permute-start(bf16[64,128,128]{2,1,0:T(8,128)(2,1)} %slice.69), channel_id=1, source_target_pairs={{0,15},{2,1},{4,3},{6,5},{8,7},{10,9},{12,11},{14,13},{16,31},{18,... | collective-permute-start | bytes 6291464 | tf_op jit(solution)/shard_map/ppermute | solution.py:198
  46.0 1.0 %copy-start.2 = (bf16[3,4,4,2,32,32]{5,2,4,1,0,3:T(4,128)(2,1)}, bf16[3,4,4,2,32,32]{5,2,4,1,0,3:T(4,128)(2,1)S(1)}, u32[]{:S(2)}) copy-start(bf16[3,4,4,2,32,32]{5,2,4,1,0,3:T(4,128)(2,1)S(1)} %copy.12) | copy-start | bytes 589828
  51.5 2.2 %copy-start = (bf16[1,128,128,128]{3,2,1,0:T(8,128)(2,1)S(1)}, bf16[1,128,128,128]{3,2,1,0:T(8,128)(2,1)}, u32[]{:S(2)}) copy-start(bf16[1,128,128,128]{3,2,1,0:T(8,128)(2,1)} %param.5) | copy-start | bytes 12582916
  53.7 9.0 %copy-start.3 = (f32[2,1]{0,1:T(1,128)S(1)}, f32[2,1]{0,1:T(1,128)}, u32[]{:S(2)}) copy-start(f32[2,1]{0,1:T(1,128)} %param.9) | copy-start | bytes 28
  53.7 9.6 %copy-start.1 = (bf16[1,128,128,128]{3,2,1,0:T(8,128)(2,1)S(1)}, bf16[1,128,128,128]{3,2,1,0:T(8,128)(2,1)}, u32[]{:S(2)}) copy-start(bf16[1,128,128,128]{3,2,1,0:T(8,128)(2,1)} %param.5) | copy-start | bytes 12582916
  62.0 18.4 %collective-permute-start.3 = (bf16[32,128,128]{2,1,0:T(8,128)(2,1)S(1)}, bf16[32,128,128]{2,1,0:T(8,128)(2,1)S(1)}, u32[]{:S(2)}, u32[]{:S(2)}) collective-permute-start(bf16[32,128,128]{2,1,0:T(8,128)(2,1)S(1)} %collective-permute-done.refs_3_), channel_id=1, source_target_pairs={{1,17},{3,19},{5,21},{7,23},{9,25},{11,27},{13,29},{15,31},{17,1},... | collective-permute-start | bytes 3145736 | tf_op jit(solution)/shard_map/ppermute | solution.py:205
  78.8 9.3 %collective-permute-start.4 = (f32[128,128]{1,0:T(8,128)S(1)}, f32[128,128]{1,0:T(8,128)S(1)}, u32[]{:S(2)}, u32[]{:S(2)}) collective-permute-start(f32[128,128]{1,0:T(8,128)S(1)} %get-tuple-element.39), channel_id=1, source_target_pairs={{0,16},{1,17},{2,18},{3,19},{4,20},{5,21},{6,22},{7,23},{8,24},{9,... | collective-permute-start | bytes 196616 | tf_op jit(solution)/shard_map/ppermute | solution.py:182
  88.8 5.8 %collective-permute-start.7 = (f32[128,128]{1,0:T(8,128)S(1)}, f32[128,128]{1,0:T(8,128)S(1)}, u32[]{:S(2)}, u32[]{:S(2)}) collective-permute-start(f32[128,128]{1,0:T(8,128)S(1)} %broadcast_multiply_fusion), channel_id=1, source_target_pairs={{0,16},{1,17},{2,18},{3,19},{4,20},{5,21},{6,22},{7,23},{8,24},{9,... | collective-permute-start | bytes 196616 | tf_op jit(solution)/shard_map/ppermute | solution.py:182
  90.7 7.3 %collective-permute-start.6 = (f32[128,128]{1,0:T(8,128)S(1)}, f32[128,128]{1,0:T(8,128)S(1)}, u32[]{:S(2)}, u32[]{:S(2)}) collective-permute-start(f32[128,128]{1,0:T(8,128)S(1)} %get-tuple-element.37), channel_id=1, source_target_pairs={{0,17},{1,18},{2,19},{3,20},{4,21},{5,22},{6,23},{7,24},{8,25},{9,... | collective-permute-start | bytes 196616 | tf_op jit(solution)/shard_map/ppermute | solution.py:182
  91.1 7.6 %collective-permute-start.5 = (f32[128,128]{1,0:T(8,128)S(1)}, f32[128,128]{1,0:T(8,128)S(1)}, u32[]{:S(2)}, u32[]{:S(2)}) collective-permute-start(f32[128,128]{1,0:T(8,128)S(1)} %get-tuple-element.38), channel_id=1, source_target_pairs={{0,1},{1,2},{2,3},{3,4},{4,5},{5,6},{6,7},{7,8},{8,9},{9,10},{10,1... | collective-permute-start | bytes 196616 | tf_op jit(solution)/shard_map/ppermute | solution.py:182

commit v6 on v5

--- a/solution.py
+++ b/solution.py
@@ -103,30 +103,35 @@
     chi_down, chi_up, held, sem = refs[2 + pieces :]
     region = held.shape[0]
 
-    def bring(moves):
-        copies = [
-            pltpu.make_async_copy(source, held.at[pl.ds(start, source.shape[0])], sem.at[i])
-            for i, (source, start) in enumerate(moves)
-        ]
-        for copy in copies:
-            copy.start()
-        for copy in copies:
-            copy.wait()
+    quarter = region // 4
+
+    def move(source, start, to, slot):
+        return pltpu.make_async_copy(
+            source.at[pl.ds(start, quarter)], held.at[pl.ds(to * quarter, quarter)], sem.at[slot]
+        )
+
+    def bring_whole():
+        for i in range(4):
+            move(parts[0], i * quarter, i, i).start()
 
     if pieces == 1:
-        bring([(parts[0], 0)])
+        bring_whole()
     else:
         t = lax.axis_index("tau")
         odd = lax.axis_index("blk") % 2
-        step = parts[1].shape[0]
-
-        @pl.when(odd == 0)
-        def _():
-            bring([(parts[0], 0)])
+        pl.when(odd == 0)(bring_whole)
 
         @pl.when(odd == 1)
         def _():
-            bring([(parts[1], t * (region - step)), (parts[2], step), (parts[3], (1 - t) * (region - step))])
+            for plane in range(2):
+
+                @pl.when(t == plane)
+                def _():
+                    first, last = (parts[1], parts[3]) if plane == 0 else (parts[3], parts[1])
+                    move(first, 0, 0, 0).start()
+                    move(parts[2], 0, 1, 1).start()
+                    move(parts[2], quarter, 2, 2).start()
+                    move(last, 0, 3, 3).start()
 
     chi_down[...] = jnp.zeros_like(chi_down)
     chi_up[...] = jnp.zeros_like(chi_up)
@@ -143,7 +148,9 @@
         chi_up[...] += lax.dot_general(flat(up), partner, dims, preferred_element_type=jnp.float32)
         return 0
 
-    lax.fori_loop(0, region // rows, body, 0)
+    for i in range(4):
+        move(parts[0], i * quarter, i, i).wait()
+        lax.fori_loop(i * quarter // rows, (i + 1) * quarter // rows, body, 0)
 
 
 def contract(down, up, parts):
@@ -156,7 +163,7 @@
         out_shape=(chi, chi),
         in_specs=[vmem] * 2 + [anywhere] * len(parts),
         out_specs=(vmem, vmem),
-        scratch_shapes=[pltpu.VMEM((region, region, width), jnp.bfloat16), pltpu.SemaphoreType.DMA((3,))],
+        scratch_shapes=[pltpu.VMEM((region, region, width), jnp.bfloat16), pltpu.SemaphoreType.DMA((4,))],
         compiler_params=pltpu.CompilerParams(vmem_limit_bytes=32 * 2**20),
         cost_estimate=pl.CostEstimate(
             flops=4 * region**2 * width**2, bytes_accessed=12 * 2**20, transcendentals=0

time: 100 us -> 99.1 us (level)
  Pallas kernels: 30.1 us -> 29.1 us
where the time goes in v6:
time: 99.1 us; the launch traced here: 98.5 us
  Pallas kernels  29.1 us (29%)
  blocking collectives  26.1 us (26%)
  local copies, waits for them, and re-layouts  19.2 us (19%)
  starting transfers between devices  13.3 us (13%)
  other arithmetic  7 us (7%)
  waiting for transfers between devices  3.53 us (4%)
    all_gather x1, blocking collectives, local(): lax.all_gather(jnp.concatenate([green_blocks[0], riders], axis=1), 'blk',...  26.1 us
    pallas_call x2, Pallas kernels, transform(): pl.pallas_call(functools.partial(transform_kernel, own_at), out_shape=sha...  22.4 us
    pallas_call x1, Pallas kernels, contract(): pl.pallas_call(functools.partial(contract_kernel, len(parts)), out_shape=...  6.75 us
    ppermute x4, starting transfers between devices, exchange(): piece = lax.ppermute(piece, ('tau', 'blk'), perm)  6.06 us
    ppermute x1, starting transfers between devices, pull_ahead(): lax.ppermute(lax.dynamic_slice_in_dim(value, start, quarter, 0), 'blk', e...  3.84 us
    ppermute x4, waiting for transfers between devices, exchange(): piece = lax.ppermute(piece, ('tau', 'blk'), perm)  3.51 us
    reshape x2, local copies, waits for them, and re-layouts, green_pairs(): blocks.reshape(count, NS, NS, 2, AB, AB).transpose(3, 0, 1, 4, 2, 5)  3.23 us
    mul x3, other arithmetic, exchange(): piece = lax.dynamic_index_in_dim(weights, target, 0, keepdims=False) * chi  3.22 us
  transfers between devices with their start and end apart: 8, of which 2 were waited for; matrix products, arithmetic and copies ran while one was open for 21% of the time, Pallas kernels for 30%

profile of v6, /device:TPU:0, one launch (start us, length us, event | category | flops | bytes accessed | tf_op | source)
XLA Modules:
  0.0 98.5 jit_solution(17059106148880329418)
XLA Ops:
  0.0 0.7 multiply_add_fusion.1
  0.8 0.8 pad_maximum_fusion
  1.6 26.1 %all_gather.3 = bf16[128,2176]{1,0:T(8,128)(2,1)} all-gather(bf16[8,2176]{1,0:T(8,128)(2,1)S(1)} %pad_maximum_fusion), channel_id=1, replica_groups=mesh['tau'=2,'blk'=16] {'blk'}, dimensions={0}, use_global_device_ids=true | all-gather | bytes 591872 | tf_op jit(solution)/shard_map/all_gather | solution.py:223
  27.7 1.3 %collective-permute-start.1 = (bf16[128,128,128]{2,1,0:T(8,128)(2,1)}, bf16[128,128,128]{2,1,0:T(8,128)(2,1)}, u32[]{:S(2)}, u32[]{:S(2)}) collective-permute-start(bf16[128,128,128]{2,1,0:T(8,128)(2,1)} %bitcast.19), channel_id=1, source_target_pairs={{1,0},{3,2},{5,4},{7,6},{9,8},{11,10},{13,12},{15,14},{17,16},{19,... | collective-permute-start | bytes 12582920 | tf_op jit(solution)/shard_map/ppermute | solution.py:206
  29.0 2.3 %constant_dynamic-slice_fusion.1 = bf16[32,128,128]{2,1,0:T(8,128)(2,1)} fusion(bf16[128,128,128]{2,1,0:T(8,128)(2,1)} %bitcast.20, s32[]{:T(128)S(6)} %select_n.30), kind=kLoop, calls=%fused_computation.15 | loop fusion | bytes 2097156 | tf_op jit(solution)/shard_map/dynamic_slice | solution.py:204
  31.3 3.8 %collective-permute-start = (bf16[32,128,128]{2,1,0:T(8,128)(2,1)}, bf16[32,128,128]{2,1,0:T(8,128)(2,1)S(1)}, u32[]{:S(2)}, u32[]{:S(2)}) collective-permute-start(bf16[32,128,128]{2,1,0:T(8,128)(2,1)} %constant_dynamic-slice_fusion.1), channel_id=1, source_target_pairs={{0,15},{2,1},{4,3},{6,5},{8,7},{10,9},{12,11},{14,13},{16,31},{18,... | collective-permute-start | bytes 3145736 | tf_op jit(solution)/shard_map/ppermute | solution.py:204
  35.1 3.2 %slice.69 = bf16[64,128,128]{2,1,0:T(8,128)(2,1)} slice(bf16[128,128,128]{2,1,0:T(8,128)(2,1)} %bitcast.21), slice={[32:96], [0:128], [0:128]} | slice | bytes 4194304 | tf_op jit(solution)/shard_map/slice | solution.py:205
  38.4 1.4 %collective-permute-start.2 = (bf16[64,128,128]{2,1,0:T(8,128)(2,1)}, bf16[64,128,128]{2,1,0:T(8,128)(2,1)S(1)}, u32[]{:S(2)}, u32[]{:S(2)}) collective-permute-start(bf16[64,128,128]{2,1,0:T(8,128)(2,1)} %slice.69), channel_id=1, source_target_pairs={{0,15},{2,1},{4,3},{6,5},{8,7},{10,9},{12,11},{14,13},{16,31},{18,... | collective-permute-start | bytes 6291464 | tf_op jit(solution)/shard_map/ppermute | solution.py:205
  39.8 0.7 dynamic-slice_convert_fusion
  40.7 2.0 %gather_fusion = bf16[48,2176]{1,0:T(8,128)(2,1)S(1)} fusion(bf16[128,2176]{1,0:T(8,128)(2,1)} %all_gather.3, s32[1024]{0:T(1024)S(1)} %pad_clamp_fusion), kind=kCustom, calls=%fused_computation | custom fusion | bytes 417984 | tf_op jit(solution)/shard_map/gather | solution.py:232
  42.8 1.5 %reshape.108 = bf16[3,4,4,2,32,32]{5,4,3,2,1,0:T(8,128)(2,1)} reshape(bf16[48,2048]{1,0:T(8,128)(2,1)S(1)} %slice.72) | data formatting | bytes 393216 | tf_op jit(solution)/shard_map/reshape | solution.py:17
  44.2 1.7 %copy.12 = bf16[3,4,4,2,32,32]{5,2,4,1,0,3:T(4,128)(2,1)S(1)} copy(bf16[3,4,4,2,32,32]{5,4,3,2,1,0:T(8,128)(2,1)} %reshape.108) | data formatting | bytes 393216 | tf_op jit(solution)/shard_map/reshape | solution.py:17
  46.0 1.0 %fusion.2 = (bf16[1,2,4,32,4,32]{5,4,3,2,1,0:T(4,128)(2,1)S(1)}, bf16[1,2,4,32,4,32]{5,4,3,2,1,0:T(4,128)(2,1)}) fusion(bf16[2,3,4,32,4,32]{5,4,3,2,1,0:T(4,128)(2,1)S(1)} %bitcast.26), kind=kLoop, calls=%fused_computation.24 | loop fusion | bytes 262144 | tf_op jit(solution)/shard_map/slice | solution.py:236
  47.2 1.7 %fusion.3 = (bf16[1,1,4,32,4,32]{5,4,3,2,1,0:T(4,128)(2,1)}, bf16[1,1,4,32,4,32]{5,4,3,2,1,0:T(4,128)(2,1)S(1)}) fusion(bf16[2,3,4,32,4,32]{5,4,3,2,1,0:T(4,128)(2,1)} %bitcast.27), kind=kLoop, calls=%fused_computation.25 | loop fusion | bytes 131072 | tf_op jit(solution)/shard_map/slice | solution.py:235
  48.9 1.0 %reshape.118 = bf16[1,128,128]{2,1,0:T(8,128)(2,1)S(1)} reshape(bf16[1,1,4,32,4,32]{5,4,3,2,1,0:T(4,128)(2,1)} %get-tuple-element.35) | data formatting | bytes 65536 | tf_op jit(solution)/shard_map/slice | solution.py:235
  50.4 1.2 %slice.66.occupied = bf16[2,128,128]{2,1,0:T(8,128)(2,1)S(1)} reshape(bf16[1,2,4,32,4,32]{5,4,3,2,1,0:T(4,128)(2,1)} %get-tuple-element.34) | data formatting | bytes 131072 | tf_op jit(solution)/shard_map/slice | solution.py:236
  51.6 2.2 %copy-done = bf16[1,128,128,128]{3,2,1,0:T(8,128)(2,1)S(1)} copy-done((bf16[1,128,128,128]{3,2,1,0:T(8,128)(2,1)S(1)}, bf16[1,128,128,128]{3,2,1,0:T(8,128)(2,1)}, u32[]{:S(2)}) %copy-start) | copy-done | bytes 4194328
  53.7 8.2 %transform.2.refs_0_ = bf16[128,128,128]{2,1,0:T(8,128)(2,1)S(1)} custom-call(bf16[1,128,128]{2,1,0:T(8,128)(2,1)S(1)} %bitcast.25, bf16[1,128,128]{2,1,0:T(8,128)(2,1)S(1)} %bitcast.24, bf16[128,128,128]{2,1,0:T(8,128)(2,1)S(1)} %bitcast.22), custom_call_target="tpu_custom_call" | custom-call | flops 3221225472 | bytes 8388608 | tf_op jit(solution)/shard_map/transform/pallas_call | solution.py:83
  62.0 0.7 collective-permute-start.3
  62.7 0.6 constant_dynamic-slice_fusion
  63.3 14.2 %transform.3 = (f32[128,128]{1,0:T(8,128)S(1)}, bf16[128,128,128]{2,1,0:T(8,128)(2,1)S(1)}) custom-call(bf16[2,128,128]{2,1,0:T(8,128)(2,1)S(1)} %slice.66.occupied, bf16[2,128,128]{2,1,0:T(8,128)(2,1)S(1)} %slice.68.virtual, bf16[128,128,128]{2,1,0:T(8,128)(2,1)S(1)} %bitcast.23), custom_call_target="tpu_custom_call" | custom-call | flops 6442450944 | bytes 8388608 | tf_op jit(solution)/shard_map/transform/pallas_call | solution.py:83
  77.5 1.3 %broadcast_multiply_fusion.2 = (f32[128,128]{1,0:T(8,128)S(1)}, f32[128,128]{1,0:T(8,128)S(1)}) fusion(f32[128,128]{1,0:T(8,128)S(1)} %get-tuple-element.28, f32[]{:T(128)} %bitcast.9, f32[]{:T(128)} %bitcast), kind=kLoop, calls=%fused_computation.7 | loop fusion | flops 32768 | bytes 196616 | tf_op jit(solution)/shard_map/mul | solution.py:182
  78.8 1.6 %collective-permute-start.4 = (f32[128,128]{1,0:T(8,128)S(1)}, f32[128,128]{1,0:T(8,128)S(1)}, u32[]{:S(2)}, u32[]{:S(2)}) collective-permute-start(f32[128,128]{1,0:T(8,128)S(1)} %get-tuple-element.39), channel_id=1, source_target_pairs={{0,16},{1,17},{2,18},{3,19},{4,20},{5,21},{6,22},{7,23},{8,24},{9,... | collective-permute-start | bytes 196616 | tf_op jit(solution)/shard_map/ppermute | solution.py:189
  80.4 6.7 %contract.1 = (f32[128,128]{1,0:T(8,128)S(1)}, f32[128,128]{1,0:T(8,128)S(1)}) custom-call(bf16[128,128,128]{2,1,0:T(8,128)(2,1)S(1)} %transform.2.refs_0_, bf16[128,128,128]{2,1,0:T(8,128)(2,1)S(1)} %get-tuple-element.24.refs_1_, bf16[128,128,128]{2,1,0:T(8,128)(2,1)} %collective-permute-done.1.refs_2_, ...), custom_call_target="tpu_custom_call" | custom-call | flops 1073741824 | bytes 12582912 | tf_op jit(solution)/shard_map/contract/pallas_call | solution.py:161
  87.1 0.7 broadcast_multiply_fusion
  88.4 1.3 %broadcast_multiply_fusion.1 = (f32[128,128]{1,0:T(8,128)S(1)}, f32[128,128]{1,0:T(8,128)S(1)}) fusion(f32[128,128]{1,0:T(8,128)S(1)} %get-tuple-element.29, f32[]{:T(128)} %bitcast.9, f32[]{:T(128)} %bitcast), kind=kLoop, calls=%fused_computation.6 | loop fusion | flops 32768 | bytes 196616 | tf_op jit(solution)/shard_map/mul | solution.py:182
  89.7 1.5 %collective-permute-start.6 = (f32[128,128]{1,0:T(8,128)S(1)}, f32[128,128]{1,0:T(8,128)S(1)}, u32[]{:S(2)}, u32[]{:S(2)}) collective-permute-start(f32[128,128]{1,0:T(8,128)S(1)} %get-tuple-element.37), channel_id=1, source_target_pairs={{0,17},{1,18},{2,19},{3,20},{4,21},{5,22},{6,23},{7,24},{8,25},{9,... | collective-permute-start | bytes 196616 | tf_op jit(solution)/shard_map/ppermute | solution.py:189
  91.2 2.4 %collective-permute-start.5 = (f32[128,128]{1,0:T(8,128)S(1)}, f32[128,128]{1,0:T(8,128)S(1)}, u32[]{:S(2)}, u32[]{:S(2)}) collective-permute-start(f32[128,128]{1,0:T(8,128)S(1)} %get-tuple-element.38), channel_id=1, source_target_pairs={{0,1},{1,2},{2,3},{3,4},{4,5},{5,6},{6,7},{7,8},{8,9},{9,10},{10,1... | collective-permute-start | bytes 196616 | tf_op jit(solution)/shard_map/ppermute | solution.py:189
  93.6 0.6 multiply_add_fusion
  94.3 2.8 %collective-permute-done.6 = f32[128,128]{1,0:T(8,128)S(1)} collective-permute-done((f32[128,128]{1,0:T(8,128)S(1)}, f32[128,128]{1,0:T(8,128)S(1)}, u32[]{:S(2)}, u32[]{:S(2)}) %collective-permute-start.6) | collective-permute-done | bytes 65568 | tf_op jit(solution)/shard_map/ppermute | solution.py:189
  97.0 0.7 collective-permute-done.5
  97.8 0.7 maximum_bitcast_fusion
  (28 shorter events, 1.5 us)
Async XLA Ops:
  27.7 52.7 %collective-permute-start.1 = (bf16[128,128,128]{2,1,0:T(8,128)(2,1)}, bf16[128,128,128]{2,1,0:T(8,128)(2,1)}, u32[]{:S(2)}, u32[]{:S(2)}) collective-permute-start(bf16[128,128,128]{2,1,0:T(8,128)(2,1)} %bitcast.19), channel_id=1, source_target_pairs={{1,0},{3,2},{5,4},{7,6},{9,8},{11,10},{13,12},{15,14},{17,16},{19,... | collective-permute-start | bytes 12582920 | tf_op jit(solution)/shard_map/ppermute | solution.py:206
  31.3 30.7 %collective-permute-start = (bf16[32,128,128]{2,1,0:T(8,128)(2,1)}, bf16[32,128,128]{2,1,0:T(8,128)(2,1)S(1)}, u32[]{:S(2)}, u32[]{:S(2)}) collective-permute-start(bf16[32,128,128]{2,1,0:T(8,128)(2,1)} %constant_dynamic-slice_fusion.1), channel_id=1, source_target_pairs={{0,15},{2,1},{4,3},{6,5},{8,7},{10,9},{12,11},{14,13},{16,31},{18,... | collective-permute-start | bytes 3145736 | tf_op jit(solution)/shard_map/ppermute | solution.py:204
  38.4 42.0 %collective-permute-start.2 = (bf16[64,128,128]{2,1,0:T(8,128)(2,1)}, bf16[64,128,128]{2,1,0:T(8,128)(2,1)S(1)}, u32[]{:S(2)}, u32[]{:S(2)}) collective-permute-start(bf16[64,128,128]{2,1,0:T(8,128)(2,1)} %slice.69), channel_id=1, source_target_pairs={{0,15},{2,1},{4,3},{6,5},{8,7},{10,9},{12,11},{14,13},{16,31},{18,... | collective-permute-start | bytes 6291464 | tf_op jit(solution)/shard_map/ppermute | solution.py:205
  46.0 1.0 %copy-start.2 = (bf16[3,4,4,2,32,32]{5,2,4,1,0,3:T(4,128)(2,1)}, bf16[3,4,4,2,32,32]{5,2,4,1,0,3:T(4,128)(2,1)S(1)}, u32[]{:S(2)}) copy-start(bf16[3,4,4,2,32,32]{5,2,4,1,0,3:T(4,128)(2,1)S(1)} %copy.12) | copy-start | bytes 589828
  51.5 2.2 %copy-start = (bf16[1,128,128,128]{3,2,1,0:T(8,128)(2,1)S(1)}, bf16[1,128,128,128]{3,2,1,0:T(8,128)(2,1)}, u32[]{:S(2)}) copy-start(bf16[1,128,128,128]{3,2,1,0:T(8,128)(2,1)} %param.5) | copy-start | bytes 12582916
  53.7 9.0 %copy-start.3 = (f32[2,1]{0,1:T(1,128)S(1)}, f32[2,1]{0,1:T(1,128)}, u32[]{:S(2)}) copy-start(f32[2,1]{0,1:T(1,128)} %param.9) | copy-start | bytes 28
  53.7 9.6 %copy-start.1 = (bf16[1,128,128,128]{3,2,1,0:T(8,128)(2,1)S(1)}, bf16[1,128,128,128]{3,2,1,0:T(8,128)(2,1)}, u32[]{:S(2)}) copy-start(bf16[1,128,128,128]{3,2,1,0:T(8,128)(2,1)} %param.5) | copy-start | bytes 12582916
  62.0 18.4 %collective-permute-start.3 = (bf16[32,128,128]{2,1,0:T(8,128)(2,1)S(1)}, bf16[32,128,128]{2,1,0:T(8,128)(2,1)S(1)}, u32[]{:S(2)}, u32[]{:S(2)}) collective-permute-start(bf16[32,128,128]{2,1,0:T(8,128)(2,1)S(1)} %collective-permute-done.refs_3_), channel_id=1, source_target_pairs={{1,17},{3,19},{5,21},{7,23},{9,25},{11,27},{13,29},{15,31},{17,1},... | collective-permute-start | bytes 3145736 | tf_op jit(solution)/shard_map/ppermute | solution.py:212
  78.8 8.3 %collective-permute-start.4 = (f32[128,128]{1,0:T(8,128)S(1)}, f32[128,128]{1,0:T(8,128)S(1)}, u32[]{:S(2)}, u32[]{:S(2)}) collective-permute-start(f32[128,128]{1,0:T(8,128)S(1)} %get-tuple-element.39), channel_id=1, source_target_pairs={{0,16},{1,17},{2,18},{3,19},{4,20},{5,21},{6,22},{7,23},{8,24},{9,... | collective-permute-start | bytes 196616 | tf_op jit(solution)/shard_map/ppermute | solution.py:189
  87.8 5.8 %collective-permute-start.7 = (f32[128,128]{1,0:T(8,128)S(1)}, f32[128,128]{1,0:T(8,128)S(1)}, u32[]{:S(2)}, u32[]{:S(2)}) collective-permute-start(f32[128,128]{1,0:T(8,128)S(1)} %broadcast_multiply_fusion), channel_id=1, source_target_pairs={{0,16},{1,17},{2,18},{3,19},{4,20},{5,21},{6,22},{7,23},{8,24},{9,... | collective-permute-start | bytes 196616 | tf_op jit(solution)/shard_map/ppermute | solution.py:189
  89.7 7.3 %collective-permute-start.6 = (f32[128,128]{1,0:T(8,128)S(1)}, f32[128,128]{1,0:T(8,128)S(1)}, u32[]{:S(2)}, u32[]{:S(2)}) collective-permute-start(f32[128,128]{1,0:T(8,128)S(1)} %get-tuple-element.37), channel_id=1, source_target_pairs={{0,17},{1,18},{2,19},{3,20},{4,21},{5,22},{6,23},{7,24},{8,25},{9,... | collective-permute-start | bytes 196616 | tf_op jit(solution)/shard_map/ppermute | solution.py:189
  91.2 6.6 %collective-permute-start.5 = (f32[128,128]{1,0:T(8,128)S(1)}, f32[128,128]{1,0:T(8,128)S(1)}, u32[]{:S(2)}, u32[]{:S(2)}) collective-permute-start(f32[128,128]{1,0:T(8,128)S(1)} %get-tuple-element.38), channel_id=1, source_target_pairs={{0,1},{1,2},{2,3},{3,4},{4,5},{5,6},{6,7},{7,8},{8,9},{9,10},{10,1... | collective-permute-start | bytes 196616 | tf_op jit(solution)/shard_map/ppermute | solution.py:189
